TPU v7x, 32 devices: a whole 2x2x4 slice. The times are simulated.
32 devices in a mesh: lat: 16 (over z, y, core), ha: 2 (over x).
Axes of the slice: x: 2, y: 2, z: 4, core: 2. Of those that a mesh axis runs over, the one named last changes fastest.
Arguments:
- adjoint_e: float32 [3, 8, 1024, 128], P(None, 'ha', 'lat'), may hold values from -6 to 6
- adjoint_h: float32 [3, 8, 1024, 128], P(None, 'ha', 'lat'), may hold values from -6 to 6
- saved_e: bfloat16 [2, 3, 8, 1024, 128], P(None, None, 'ha', 'lat'), may hold values from -5 to 5
- labels: int32 [8, 1024, 128], P('ha', 'lat'), may hold values from 0 to 3
- eps_table: float32 [4], replicated, may hold values from 1 to 12
- chi_table: float32 [4], replicated, may hold values from 0.05 to 0.5
- density: float32 [1024, 128], P('lat'), may hold values from 0 to 1
- mon_cells: int32 [16384], P(('lat', 'ha')), may hold values from 0 to 32767
- mon_weight: float32 [16384], P(('lat', 'ha')), may hold values from 0.25 to 6.75
Outputs:
- final_e: float32 [3, 8, 1024, 128], P(None, 'ha', 'lat')
- final_h: float32 [3, 8, 1024, 128], P(None, 'ha', 'lat')
- design_grad: float32 [1024, 128], P('lat')
Inputs may be any that keep to these rules, and one draw needn't show every extreme that they name: `labels`: label 0 marks design cells. `mon_cells`: entry m names a cell of the block of block number m // 512 (lat major, ha minor), numbered in z, x, y order within the block; entries may repeat.
All inputs are finite; a program needn't handle non-finite values.
Results may differ from a plain program's by a relative error of at most 0.0003.
Values sent between devices are 32-bit elements; how exact they have to be, the bound alone decides.
A program may use at most 64 MiB of HBM per device.

v0:
```python
import jax
import jax.numpy as jnp
from jax import lax
from jax.sharding import PartitionSpec as P

RADIUS = 16


sharpness = 8.0
threshold = 0.5
time_step = 0.5
epsilon = 1e-05


def passed_along(value, axis, steps):
    count = lax.axis_size(axis)
    first, last = (max(0, -steps), min(count, count - steps))
    return lax.ppermute(value, axis, [(source, source + steps) for source in range(first, last)])


def extended(cells, sides, width):
    for axis, dim in sides:
        count = lax.axis_size(axis)
        ends = count - 1
        head = lax.slice_in_dim(cells, 0, width, axis=dim)
        tail = lax.slice_in_dim(cells, cells.shape[dim] - width, cells.shape[dim], axis=dim)
        cells = jnp.concatenate(
            [
                lax.ppermute(tail, axis, [(i, (i + 1) % count) for i in range(ends)]),
                cells,
                lax.ppermute(head, axis, [((i + 1) % count, i) for i in range(ends)]),
            ],
            axis=dim,
        )
    return cells


def below_height(field, plane):
    return jnp.concatenate([plane[None], field[:-1]], 0)


def below_side(field, plane):
    return jnp.concatenate([plane[:, None], field[:, :-1]], 1)


def below_across(field):
    return jnp.concatenate([jnp.zeros_like(field[:, :, :1]), field[:, :, :-1]], 2)


def above_height(field, plane):
    return jnp.concatenate([field[1:], plane[None]], 0)


def above_side(field, plane):
    return jnp.concatenate([field[:, 1:], plane[:, None]], 1)


def above_across(field):
    return jnp.concatenate([field[:, :, 1:], jnp.zeros_like(field[:, :, :1])], 2)


def lower_planes(scaled):
    height_send = scaled[0:2, -1]
    side_send = scaled[1:3, :, -1]
    height_recv = passed_along(height_send, "ha", 1)
    side_recv = passed_along(side_send, "lat", 1)
    result = (height_recv, side_recv)
    return result


def upper_planes(field):
    height_send = field[0:2, 0]
    side_send = field[1:3, :, 0]
    height_recv = passed_along(height_send, "ha", -1)
    side_recv = passed_along(side_send, "lat", -1)
    result = (height_recv, side_recv)
    return result


def curl_lower(scaled):
    height_plane, side_plane = lower_planes(scaled)
    field_x, field_y, field_z = (scaled[0], scaled[1], scaled[2])
    curl_x = field_z - below_across(field_z) - (field_y - below_height(field_y, height_plane[1]))
    curl_y = (
        field_x
        - below_height(field_x, height_plane[0])
        - (field_z - below_side(field_z, side_plane[1]))
    )
    curl_z = field_y - below_side(field_y, side_plane[0]) - (field_x - below_across(field_x))
    return jnp.stack([curl_x, curl_y, curl_z])


def curl_upper(field):
    height_plane, side_plane = upper_planes(field)
    field_x, field_y, field_z = (field[0], field[1], field[2])
    curl_x = above_across(field_z) - field_z - (above_height(field_y, height_plane[1]) - field_y)
    curl_y = (
        above_height(field_x, height_plane[0])
        - field_x
        - (above_side(field_z, side_plane[1]) - field_z)
    )
    curl_z = above_side(field_y, side_plane[0]) - field_y - (above_across(field_x) - field_x)
    return jnp.stack([curl_x, curl_y, curl_z])


def cone(offset):
    return jnp.maximum(RADIUS + 1 - jnp.abs(offset), 0).astype(jnp.float32) / (RADIUS + 1) ** 2


def filter_rows(padded, rows):
    col_index = jnp.arange(padded.shape[1])
    across = cone(col_index[:, None] - col_index[None, :])
    smoothed = jnp.dot(
        padded, across, precision=lax.Precision.HIGHEST, preferred_element_type=jnp.float32
    )
    row_out = jnp.arange(rows)
    row_in = jnp.arange(rows + 2 * RADIUS)
    downward = cone(row_in[None, :] - RADIUS - row_out[:, None])
    return jnp.dot(
        downward, smoothed, precision=lax.Precision.HIGHEST, preferred_element_type=jnp.float32
    )


def body(
    adjoint_e, adjoint_h, saved_e, labels, eps_table, chi_table, density, mon_cells, mon_weight
):
    eps_cell = jnp.zeros(labels.shape, jnp.float32)
    chi_cell = jnp.zeros(labels.shape, jnp.float32)
    for region in range(eps_table.shape[0]):
        member = (labels == region).astype(jnp.float32)
        eps_cell = eps_cell + member * eps_table[region]
        chi_cell = chi_cell + member * chi_table[region]
    design = (labels == 0).astype(jnp.float32)
    count_all = mon_cells.shape[0] * lax.axis_size("lat") * lax.axis_size("ha")
    steps_total = saved_e.shape[0]
    shape = adjoint_e.shape
    lam_e = adjoint_e
    lam_h = adjoint_h
    plane = jnp.zeros((shape[2], shape[3]), jnp.float32)
    for index in reversed(range(steps_total)):
        forward = saved_e[index].astype(jnp.float32)
        jacobian = eps_cell[None] + 3.0 * chi_cell[None] * forward * forward
        picked = saved_e[index].reshape(3, -1)[:, mon_cells].astype(jnp.float32)
        term = jnp.sum(mon_weight * jnp.sum(picked * picked, 0))
        power = lax.psum(term, ("lat", "ha")) / count_all + epsilon
        lam_e = (
            lam_e.reshape(3, -1).at[:, mon_cells].add(mon_weight * picked / power).reshape(shape)
        )
        scaled = lam_e / jacobian
        plane = plane + jnp.sum(design * jnp.sum(scaled * forward, 0), 0)
        lam_h = lam_h - time_step * curl_lower(scaled)
        lam_e = lam_e + time_step * curl_upper(lam_h)
    extruded = lax.psum(plane, "ha")
    rows = density.shape[0]
    padded_density = extended(density, (("lat", 0),), RADIUS)
    filtered = filter_rows(padded_density, rows)
    slope = jnp.tanh(sharpness * (filtered - threshold))
    derivative = (
        sharpness
        * (1.0 - slope * slope)
        / (jnp.tanh(sharpness * threshold) + jnp.tanh(sharpness * (1.0 - threshold)))
    )
    product = derivative * extruded
    padded_product = extended(product, (("lat", 0),), RADIUS)
    return (lam_e, lam_h, filter_rows(padded_product, rows))


def solution(mesh):
    return jax.shard_map(
        body,
        mesh=mesh,
        in_specs=(
            P(None, "ha", "lat", None),
            P(None, "ha", "lat", None),
            P(None, None, "ha", "lat", None),
            P("ha", "lat", None),
            P(),
            P(),
            P("lat", None),
            P(("lat", "ha")),
            P(("lat", "ha")),
        ),
        out_specs=(P(None, "ha", "lat", None), P(None, "ha", "lat", None), P("lat", None)),
        check_vma=False,
    )
```

profile of v0, /device:TPU:0, one launch (start us, length us, event | category | flops | bytes accessed | tf_op | source)
XLA Modules:
  0.0 220.8 jit_solution(5407053460315099079)
XLA Ops:
  2.5 5.8 %copy.104 = bf16[3,32768]{0,1:T(8,128)(2,1)} copy(bf16[3,32768]{1,0:T(4,128)(2,1)S(1)} %reshape_squeeze.6) | data formatting | bytes 393216 | tf_op jit(solution)/shard_map/reshape;squeeze | solution.py:143
  8.3 5.5 %gather_fusion = bf16[512,3]{1,0:T(8,128)(2,1)S(1)} fusion(bf16[3,32768]{0,1:T(8,128)(2,1)} %copy.104, s32[1024]{0:T(1024)S(1)} %pad_clamp_fusion), kind=kCustom, calls=%fused_computation | custom fusion | bytes 8192 | tf_op jit(solution)/shard_map/gather | solution.py:143
  14.0 5.8 %copy.115 = bf16[3,32768]{0,1:T(8,128)(2,1)} copy(bf16[3,32768]{1,0:T(4,128)(2,1)S(1)} %reshape_squeeze.7) | data formatting | bytes 393216 | tf_op jit(solution)/shard_map/reshape;squeeze | solution.py:143
  19.8 5.5 %gather_fusion.1 = bf16[512,3]{1,0:T(8,128)(2,1)S(1)} fusion(bf16[3,32768]{0,1:T(8,128)(2,1)} %copy.115, s32[1024]{0:T(1024)S(1)} %pad_clamp_fusion), kind=kCustom, calls=%fused_computation.1 | custom fusion | bytes 8192 | tf_op jit(solution)/shard_map/gather | solution.py:143
  26.1 42.3 %all-reduce.8 = (f32[]{:T(128)}, f32[]{:T(128)}) all-reduce(f32[]{:T(128)} %get-tuple-element.14, f32[]{:T(128)} %get-tuple-element.13), channel_id=1, replica_groups=mesh['lat'=16,'ha'=2] {'lat','ha'}, use_global_device_ids=true, to_apply=%region_2.0 | all-reduce | flops 2 | bytes 16 | tf_op jit(solution)/shard_map/psum | solution.py:145
  69.9 8.6 %copy.103 = f32[3,4,64,128]{0,3,2,1:T(8,128)} copy(f32[3,4,64,128]{3,2,1,0:T(8,128)S(1)} %copy-done.5) | data formatting | bytes 786432 | tf_op args[0]
  78.5 14.5 %scatter_fusion = f32[3,32768]{0,1:T(8,128)} fusion(f32[3,32768]{0,1:T(8,128)} %bitcast.173, s32[512]{0:T(512)S(1)} %compare_select_fusion, f32[512,3]{1,0:T(8,128)S(1)} %copy.106), kind=kCustom, calls=%fused_computation.2 | custom fusion | flops 1536 | bytes 20480 | tf_op jit(solution)/shard_map/scatter-add | solution.py:147
  93.0 10.0 %copy.128 = f32[3,4,64,128]{3,2,1,0:T(8,128)S(1)} copy(f32[3,4,64,128]{0,3,2,1:T(8,128)} %bitcast.174) | data formatting | bytes 786432 | tf_op jit(solution)/shard_map/reshape | solution.py:147
  104.3 2.7 %select_add_fusion = (f32[4,64,128]{2,1,0:T(8,128)S(1)}, pred[4,64,128]{2,1,0:T(8,128)(4,1)S(1)}, pred[4,64,128]{2,1,0:T(8,128)(4,1)S(1)}, pred[4,64,128]{2,1,0:T(8,128)(4,1)S(1)}, pred[4,64,128]{2,1,0:T(8,128)(4,1)S(1)}) fusion(f32[]{:T(128)} %bitcast.5, f32[]{:T(128)} %bitcast.4, f32[]{:T(128)} %bitcast.3, f32[]{:T(128)} %bitcast.2, ...), kind=kLoop, calls=%fused_computation.80 | loop fusion | flops 360448 | bytes 393232 | tf_op jit(solution)/shard_map/add | solution.py:131
  107.1 2.6 %add_multiply_fusion = f32[4,64,128]{2,1,0:T(8,128)S(1)} fusion(pred[4,64,128]{2,1,0:T(8,128)(4,1)S(1)} %get-tuple-element.21, pred[4,64,128]{2,1,0:T(8,128)(4,1)S(1)} %get-tuple-element.20, pred[4,64,128]{2,1,0:T(8,128)(4,1)S(1)} %get-tuple-element.19, pred[4,64,128]{2,1,0:T(8,128)(4,1)S(1)} %get-tuple-element.18, f32[]{:T(128)} %bitcast.9, f32[]{:T(128)} %bitcast.8, ...), kind=kLoop, calls=%fused_computation.79 | loop fusion | flops 262144 | bytes 262160 | tf_op jit(solution)/shard_map/mul | solution.py:142
  109.8 4.2 %collective-permute-start = (f32[2,64,128]{2,1,0:T(8,128)S(1)}, f32[2,64,128]{2,1,0:T(8,128)S(1)}, u32[]{:S(2)}, u32[]{:S(2)}) collective-permute-start(f32[2,64,128]{2,1,0:T(8,128)S(1)} %slice_bitcast_fusion.23), channel_id=1, source_target_pairs={{0,1},{2,3},{4,5},{6,7},{8,9},{10,11},{12,13},{14,15},{16,17},{18,... | collective-permute-start | bytes 196616 | tf_op jit(solution)/shard_map/ppermute | solution.py:18
  115.3 3.4 %collective-permute-start.8 = (f32[16,128]{1,0:T(8,128)S(1)}, f32[16,128]{1,0:T(8,128)S(1)}, u32[]{:S(2)}, u32[]{:S(2)}) collective-permute-start(f32[16,128]{1,0:T(8,128)S(1)} %get-tuple-element.62), channel_id=1, source_target_pairs={{0,2},{2,4},{4,6},{6,8},{8,10},{10,12},{12,14},{14,16},{16,18},{18... | collective-permute-start | bytes 24584 | tf_op jit(solution)/shard_map/ppermute | solution.py:29
  120.1 9.5 %copy.114 = f32[3,32768]{1,0:T(4,128)S(1)} copy(f32[3,32768]{0,1:T(8,128)} %scatter_fusion) | data formatting | bytes 786432 | tf_op jit(solution)/shard_map/scatter-add | solution.py:147
  131.6 1.3 collective-permute-start.3
  133.0 1.5 collective-permute-start.2
  135.3 3.9 %collective-permute-done.2 = f32[2,64,128]{2,1,0:T(8,128)S(1)} collective-permute-done((f32[2,64,128]{2,1,0:T(8,128)S(1)}, f32[2,64,128]{2,1,0:T(8,128)S(1)}, u32[]{:S(2)}, u32[]{:S(2)}) %collective-permute-start.2) | collective-permute-done | bytes 65568 | tf_op jit(solution)/shard_map/ppermute | solution.py:18
  139.9 8.5 %copy.117 = f32[3,32768]{0,1:T(8,128)} copy(f32[3,32768]{1,0:T(4,128)S(1)} %fusion.12) | data formatting | bytes 786432 | tf_op jit(solution)/shard_map/add | solution.py:152
  148.4 14.9 %scatter_fusion.1 = f32[3,32768]{0,1:T(8,128)} fusion(f32[3,32768]{0,1:T(8,128)} %copy.117, s32[512]{0:T(512)S(1)} %compare_select_fusion, f32[512,3]{1,0:T(8,128)} %copy.118), kind=kCustom, calls=%fused_computation.3 | custom fusion | flops 1536 | bytes 20480 | tf_op jit(solution)/shard_map/scatter-add | solution.py:147
  163.3 9.5 %copy.127 = f32[3,32768]{1,0:T(4,128)S(1)} copy(f32[3,32768]{0,1:T(8,128)} %scatter_fusion.1) | data formatting | bytes 786432 | tf_op jit(solution)/shard_map/scatter-add | solution.py:147
  172.8 10.0 %copy.129 = f32[3,4,64,128]{3,2,1,0:T(8,128)S(1)} copy(f32[3,4,64,128]{0,3,2,1:T(8,128)} %bitcast.172) | data formatting | bytes 786432 | tf_op jit(solution)/shard_map/reshape | solution.py:147
  185.4 7.0 %psum.23 = f32[64,128]{1,0:T(8,128)S(1)} all-reduce(f32[64,128]{1,0:T(8,128)S(1)} %add.115), channel_id=1, replica_groups=mesh['lat'=16,'ha'=2] {'ha'}, use_global_device_ids=true, to_apply=%region_12.0 | all-reduce | flops 8192 | bytes 65536 | tf_op jit(solution)/shard_map/psum | solution.py:153
  194.8 6.3 %collective-permute-start.5 = (f32[2,4,128]{2,1,0:T(4,128)S(1)}, f32[2,4,128]{2,1,0:T(4,128)S(1)}, u32[]{:S(2)}, u32[]{:S(2)}) collective-permute-start(f32[2,4,128]{2,1,0:T(4,128)S(1)} %bitcast.196), channel_id=1, source_target_pairs={{0,2},{2,4},{4,6},{6,8},{8,10},{10,12},{12,14},{14,16},{16,18},{18... | collective-permute-start | bytes 12296 | tf_op jit(solution)/shard_map/ppermute | solution.py:18
  202.4 4.0 %collective-permute-start.4 = (f32[2,64,128]{2,1,0:T(8,128)S(1)}, f32[2,64,128]{2,1,0:T(8,128)S(1)}, u32[]{:S(2)}, u32[]{:S(2)}) collective-permute-start(f32[2,64,128]{2,1,0:T(8,128)S(1)} %slice_bitcast_fusion.21), channel_id=1, source_target_pairs={{0,1},{2,3},{4,5},{6,7},{8,9},{10,11},{12,13},{14,15},{16,17},{18,... | collective-permute-start | bytes 196616 | tf_op jit(solution)/shard_map/ppermute | solution.py:18
  214.8 4.9 %collective-permute-done.6 = f32[2,64,128]{2,1,0:T(8,128)S(1)} collective-permute-done((f32[2,64,128]{2,1,0:T(8,128)S(1)}, f32[2,64,128]{2,1,0:T(8,128)S(1)}, u32[]{:S(2)}, u32[]{:S(2)}) %collective-permute-start.6) | collective-permute-done | bytes 65568 | tf_op jit(solution)/shard_map/ppermute | solution.py:18
  (112 shorter events, 26.1 us)
Async XLA Ops:
  0.6 24.8 %copy-start.8 = (f32[512]{0:T(512)S(1)}, f32[512]{0:T(512)}, u32[]{:S(2)}) copy-start(f32[512]{0:T(512)} %param.17) | copy-start | bytes 6148
  0.6 69.2 %copy-start.5 = (f32[3,4,64,128]{3,2,1,0:T(8,128)S(1)}, f32[3,4,64,128]{3,2,1,0:T(8,128)}, u32[]{:S(2)}) copy-start(f32[3,4,64,128]{3,2,1,0:T(8,128)} %param.9) | copy-start | bytes 1179652
  69.8 33.2 %copy-start.10 = (f32[4]{0:T(128)S(1)}, f32[4]{0:T(128)}, u32[]{:S(2)}) copy-start(f32[4]{0:T(128)} %param.13) | copy-start | bytes 52
  69.8 33.9 %copy-start.11 = (f32[4]{0:T(128)S(1)}, f32[4]{0:T(128)}, u32[]{:S(2)}) copy-start(f32[4]{0:T(128)} %param.14) | copy-start | bytes 52
  69.8 34.5 %copy-start.7 = (s32[4,64,128]{2,1,0:T(8,128)S(1)}, s32[4,64,128]{2,1,0:T(8,128)}, u32[]{:S(2)}) copy-start(s32[4,64,128]{2,1,0:T(8,128)} %param.12) | copy-start | bytes 393220
  69.9 39.8 %copy-start.1 = (bf16[2,3,4,64,128]{4,3,2,1,0:T(8,128)(2,1)S(1)}, bf16[2,3,4,64,128]{4,3,2,1,0:T(8,128)(2,1)}, u32[]{:S(2)}) copy-start(bf16[2,3,4,64,128]{4,3,2,1,0:T(8,128)(2,1)} %param.11) | copy-start | bytes 1179652
  69.9 45.4 %copy-start.9 = (f32[64,128]{1,0:T(8,128)S(1)}, f32[64,128]{1,0:T(8,128)}, u32[]{:S(2)}) copy-start(f32[64,128]{1,0:T(8,128)} %param.15) | copy-start | bytes 98308
  93.0 38.5 %copy-start.2 = (f32[3,4,64,128]{3,2,1,0:T(8,128)S(1)}, f32[3,4,64,128]{3,2,1,0:T(8,128)}, u32[]{:S(2)}) copy-start(f32[3,4,64,128]{3,2,1,0:T(8,128)} %param.10) | copy-start | bytes 1179652
  107.1 12.9 %copy-start.6 = (pred[4,64,128]{2,1,0:T(8,128)(4,1)}, pred[4,64,128]{2,1,0:T(8,128)(4,1)S(1)}, u32[]{:S(2)}) copy-start(pred[4,64,128]{2,1,0:T(8,128)(4,1)S(1)} %get-tuple-element.18) | copy-start | bytes 98308
  109.8 21.5 %collective-permute-start = (f32[2,64,128]{2,1,0:T(8,128)S(1)}, f32[2,64,128]{2,1,0:T(8,128)S(1)}, u32[]{:S(2)}, u32[]{:S(2)}) collective-permute-start(f32[2,64,128]{2,1,0:T(8,128)S(1)} %slice_bitcast_fusion.23), channel_id=1, source_target_pairs={{0,1},{2,3},{4,5},{6,7},{8,9},{10,11},{12,13},{14,15},{16,17},{18,... | collective-permute-start | bytes 196616 | tf_op jit(solution)/shard_map/ppermute | solution.py:18
  114.0 16.4 %collective-permute-start.1 = (f32[2,4,128]{2,1,0:T(4,128)S(1)}, f32[2,4,128]{2,1,0:T(4,128)S(1)}, u32[]{:S(2)}, u32[]{:S(2)}) collective-permute-start(f32[2,4,128]{2,1,0:T(4,128)S(1)} %bitcast.197), channel_id=1, source_target_pairs={{0,2},{2,4},{4,6},{6,8},{8,10},{10,12},{12,14},{14,16},{16,18},{18... | collective-permute-start | bytes 12296 | tf_op jit(solution)/shard_map/ppermute | solution.py:18
  115.3 15.1 %collective-permute-start.8 = (f32[16,128]{1,0:T(8,128)S(1)}, f32[16,128]{1,0:T(8,128)S(1)}, u32[]{:S(2)}, u32[]{:S(2)}) collective-permute-start(f32[16,128]{1,0:T(8,128)S(1)} %get-tuple-element.62), channel_id=1, source_target_pairs={{0,2},{2,4},{4,6},{6,8},{8,10},{10,12},{12,14},{14,16},{16,18},{18... | collective-permute-start | bytes 24584 | tf_op jit(solution)/shard_map/ppermute | solution.py:29
  118.7 11.7 %collective-permute-start.9 = (f32[16,128]{1,0:T(8,128)S(1)}, f32[16,128]{1,0:T(8,128)S(1)}, u32[]{:S(2)}, u32[]{:S(2)}) collective-permute-start(f32[16,128]{1,0:T(8,128)S(1)} %get-tuple-element.63), channel_id=1, source_target_pairs={{2,0},{4,2},{6,4},{8,6},{10,8},{12,10},{14,12},{16,14},{18,16},{20... | collective-permute-start | bytes 24584 | tf_op jit(solution)/shard_map/ppermute | solution.py:31
  131.3 41.5 %copy-start.4 = (f32[1,4,64,128]{3,2,1,0:T(8,128)}, f32[1,4,64,128]{3,2,1,0:T(8,128)S(1)}, u32[]{:S(2)}) copy-start(f32[1,4,64,128]{3,2,1,0:T(8,128)S(1)} %get-tuple-element.47) | copy-start | bytes 393220
  131.5 41.3 %copy-start.3 = (f32[1,4,64,128]{3,2,1,0:T(8,128)}, f32[1,4,64,128]{3,2,1,0:T(8,128)S(1)}, u32[]{:S(2)}) copy-start(f32[1,4,64,128]{3,2,1,0:T(8,128)S(1)} %get-tuple-element.44) | copy-start | bytes 393220
  131.6 3.7 %collective-permute-start.3 = (f32[2,4,128]{2,1,0:T(4,128)S(1)}, f32[2,4,128]{2,1,0:T(4,128)S(1)}, u32[]{:S(2)}, u32[]{:S(2)}) collective-permute-start(f32[2,4,128]{2,1,0:T(4,128)S(1)} %bitcast.198), channel_id=1, source_target_pairs={{2,0},{4,2},{6,4},{8,6},{10,8},{12,10},{14,12},{16,14},{18,16},{20... | collective-permute-start | bytes 12296 | tf_op jit(solution)/shard_map/ppermute | solution.py:18
  133.0 6.2 %collective-permute-start.2 = (f32[2,64,128]{2,1,0:T(8,128)S(1)}, f32[2,64,128]{2,1,0:T(8,128)S(1)}, u32[]{:S(2)}, u32[]{:S(2)}) collective-permute-start(f32[2,64,128]{2,1,0:T(8,128)S(1)} %slice_bitcast_fusion.22), channel_id=1, source_target_pairs={{1,0},{3,2},{5,4},{7,6},{9,8},{11,10},{13,12},{15,14},{17,16},{19,... | collective-permute-start | bytes 196616 | tf_op jit(solution)/shard_map/ppermute | solution.py:18
  193.5 12.9 %collective-permute-start.10 = (f32[16,128]{1,0:T(8,128)S(1)}, f32[16,128]{1,0:T(8,128)S(1)}, u32[]{:S(2)}, u32[]{:S(2)}) collective-permute-start(f32[16,128]{1,0:T(8,128)S(1)} %get-tuple-element.60), channel_id=1, source_target_pairs={{0,2},{2,4},{4,6},{6,8},{8,10},{10,12},{12,14},{14,16},{16,18},{18... | collective-permute-start | bytes 24584 | tf_op jit(solution)/shard_map/ppermute | solution.py:29
  194.8 11.6 %collective-permute-start.5 = (f32[2,4,128]{2,1,0:T(4,128)S(1)}, f32[2,4,128]{2,1,0:T(4,128)S(1)}, u32[]{:S(2)}, u32[]{:S(2)}) collective-permute-start(f32[2,4,128]{2,1,0:T(4,128)S(1)} %bitcast.196), channel_id=1, source_target_pairs={{0,2},{2,4},{4,6},{6,8},{8,10},{10,12},{12,14},{14,16},{16,18},{18... | collective-permute-start | bytes 12296 | tf_op jit(solution)/shard_map/ppermute | solution.py:18
  201.1 5.3 %collective-permute-start.11 = (f32[16,128]{1,0:T(8,128)S(1)}, f32[16,128]{1,0:T(8,128)S(1)}, u32[]{:S(2)}, u32[]{:S(2)}) collective-permute-start(f32[16,128]{1,0:T(8,128)S(1)} %get-tuple-element.61), channel_id=1, source_target_pairs={{2,0},{4,2},{6,4},{8,6},{10,8},{12,10},{14,12},{16,14},{18,16},{20... | collective-permute-start | bytes 24584 | tf_op jit(solution)/shard_map/ppermute | solution.py:31
  202.4 6.3 %collective-permute-start.4 = (f32[2,64,128]{2,1,0:T(8,128)S(1)}, f32[2,64,128]{2,1,0:T(8,128)S(1)}, u32[]{:S(2)}, u32[]{:S(2)}) collective-permute-start(f32[2,64,128]{2,1,0:T(8,128)S(1)} %slice_bitcast_fusion.21), channel_id=1, source_target_pairs={{0,1},{2,3},{4,5},{6,7},{8,9},{10,11},{12,13},{14,15},{16,17},{18,... | collective-permute-start | bytes 196616 | tf_op jit(solution)/shard_map/ppermute | solution.py:18
  211.7 9.1 %copy-start = (f32[3,4,64,128]{3,2,1,0:T(8,128)}, f32[3,4,64,128]{3,2,1,0:T(8,128)S(1)}, u32[]{:S(2)}) copy-start(f32[3,4,64,128]{3,2,1,0:T(8,128)S(1)} %fusion.18) | copy-start | bytes 1179652
  211.8 3.1 %collective-permute-start.7 = (f32[2,4,128]{2,1,0:T(4,128)S(1)}, f32[2,4,128]{2,1,0:T(4,128)S(1)}, u32[]{:S(2)}, u32[]{:S(2)}) collective-permute-start(f32[2,4,128]{2,1,0:T(4,128)S(1)} %bitcast.199), channel_id=1, source_target_pairs={{2,0},{4,2},{6,4},{8,6},{10,8},{12,10},{14,12},{16,14},{18,16},{20... | collective-permute-start | bytes 12296 | tf_op jit(solution)/shard_map/ppermute | solution.py:18
  213.2 6.6 %collective-permute-start.6 = (f32[2,64,128]{2,1,0:T(8,128)S(1)}, f32[2,64,128]{2,1,0:T(8,128)S(1)}, u32[]{:S(2)}, u32[]{:S(2)}) collective-permute-start(f32[2,64,128]{2,1,0:T(8,128)S(1)} %slice_bitcast_fusion.20), channel_id=1, source_target_pairs={{1,0},{3,2},{5,4},{7,6},{9,8},{11,10},{13,12},{15,14},{17,16},{19,... | collective-permute-start | bytes 196616 | tf_op jit(solution)/shard_map/ppermute | solution.py:18
where the time goes:
time: 223 us; the launch traced here: 221 us
  local copies, waits for them, and re-layouts  83.8 us (38%)
  blocking collectives  49.3 us (22%)
  other arithmetic  42.8 us (19%)
  starting transfers between devices  28.3 us (13%)
  waiting for transfers between devices  11.2 us (5%)
  matrix products  2.8 us (1%)
  between operations  2.65 us (1%)
    psum x1, blocking collectives, body(): power = lax.psum(term, ('lat', 'ha')) / count_all + epsilon  42.3 us
    scatter-add x2, other arithmetic, body(): lam_e.reshape(3, -1).at[:, mon_cells].add(mon_weight * picked / power)  29.4 us
    ppermute x8, starting transfers between devices, passed_along(): lax.ppermute(value, axis, [(source, source + steps) for source in range(f...  21.1 us
    reshape x2, local copies, waits for them, and re-layouts, body(): lam_e.reshape(3, -1).at[:, mon_cells].add(mon_weight * picked / power)  20 us
    scatter-add x2, local copies, waits for them, and re-layouts, body(): lam_e.reshape(3, -1).at[:, mon_cells].add(mon_weight * picked / power)  18.9 us
    another operation x4, local copies, waits for them, and re-layouts, body(): picked = saved_e[index].reshape(3, -1)[:, mon_cells].astype(jnp.float32)  11.7 us
    gather x4, local copies, waits for them, and re-layouts, body(): picked = saved_e[index].reshape(3, -1)[:, mon_cells].astype(jnp.float32)  11.2 us
    ppermute x8, waiting for transfers between devices, passed_along(): lax.ppermute(value, axis, [(source, source + steps) for source in range(f...  11.2 us
  transfers between devices with their start and end apart: 12, of which 5 were waited for; matrix products, arithmetic and copies ran while one was open for 6% of the time, Pallas kernels for 0%

commit v1 on v0

v1 whole, which is shorter than its diff:
```python
import functools

import jax
import jax.numpy as jnp
from jax import lax
from jax.experimental import pallas as pl
from jax.experimental.pallas import tpu as pltpu
from jax.sharding import PartitionSpec as P

RADIUS = 16

sharpness = 8.0
threshold = 0.5
time_step = 0.5
epsilon = 1e-05

MESH = pl.DeviceIdType.MESH


def cone(offset):
    return jnp.maximum(RADIUS + 1 - jnp.abs(offset), 0).astype(jnp.float32) / (RADIUS + 1) ** 2


def filter_rows(padded, rows):
    width = padded.shape[1]
    i = lax.broadcasted_iota(jnp.int32, (width, width), 0)
    j = lax.broadcasted_iota(jnp.int32, (width, width), 1)
    smoothed = jnp.dot(
        padded, cone(i - j), precision=lax.Precision.HIGHEST, preferred_element_type=jnp.float32
    )
    row_out = lax.broadcasted_iota(jnp.int32, (rows, rows + 2 * RADIUS), 0)
    row_in = lax.broadcasted_iota(jnp.int32, (rows, rows + 2 * RADIUS), 1)
    return jnp.dot(
        cone(row_in - RADIUS - row_out),
        smoothed,
        precision=lax.Precision.HIGHEST,
        preferred_element_type=jnp.float32,
    )


def kernel(
    n_lat,
    n_ha,
    adj_e,
    adj_h,
    saved,
    labels,
    eps_table,
    chi_table,
    density,
    cells,
    weight,
    out_e,
    out_h,
    out_g,
    e,
    h0,
    sv,
    lb,
    dens,
    cl,
    wt,
    wgrid,
    ab,
    s,
    hh,
    rinv,
    plane,
    grad,
    dens_lo,
    dens_hi,
    deriv,
    zab,
    rab_out,
    rab,
    zl,
    rl_out,
    rl,
    zu,
    ru_out,
    ru,
    pw_out,
    pw_ha,
    pw_sum,
    pw_lat,
    plane_ha,
    plane_lo,
    plane_hi,
    local_sem,
    send_sem,
    recv_sem,
):
    steps, comps, depth, rows, width = sv.shape
    regions = eps_table.shape[0]
    entries = cl.shape[1]
    lat = lax.axis_index("lat")
    ha = lax.axis_index("ha")
    lat_dn, lat_up = lat > 0, lat < n_lat - 1
    ha_dn, ha_up = ha > 0, ha < n_ha - 1
    lat_prev, lat_next = jnp.maximum(lat - 1, 0), jnp.minimum(lat + 1, n_lat - 1)
    ha_prev, ha_next = jnp.maximum(ha - 1, 0), jnp.minimum(ha + 1, n_ha - 1)

    pairs = [
        (cells, cl),
        (weight, wt),
        (saved, sv),
        (adj_e, e),
        (labels, lb),
        (density, dens),
        (adj_h, h0),
    ]
    loads = [pltpu.make_async_copy(a, b, local_sem.at[i]) for i, (a, b) in enumerate(pairs)]
    for load in loads:
        load.start()

    barrier = pltpu.get_barrier_semaphore()

    def greet(l, k):
        pl.semaphore_signal(barrier, inc=1, device_id=(l, k), device_id_type=MESH)

    for d in range(1, n_lat):
        greet(lax.rem(lat + d, n_lat), ha)
    for d in range(1, n_ha):
        other = lax.rem(ha + d, n_ha)
        greet(lat, other)
        pl.when(lat_dn)(functools.partial(greet, lat_prev, other))
        pl.when(lat_up)(functools.partial(greet, lat_next, other))

    issued = []

    def exchange(src, dst, target, sends=None, receives=None):
        index = len(issued)

        def copy():
            return pltpu.make_async_remote_copy(
                src_ref=src,
                dst_ref=dst,
                send_sem=send_sem.at[index],
                recv_sem=recv_sem.at[index],
                device_id=target,
                device_id_type=MESH,
            )

        def guarded(condition, action):
            if condition is None:
                action()
            else:
                pl.when(condition)(action)

        issued.append(lambda: guarded(sends, lambda: copy().wait_send()))
        guarded(sends, lambda: copy().start())

        def arrive():
            guarded(receives, lambda: copy().wait_recv())
            if receives is not None:

                @pl.when(jnp.logical_not(receives))
                def _():
                    dst[...] = jnp.zeros(dst.shape, dst.dtype)

        return arrive

    loads[0].wait()
    loads[1].wait()
    cell = cl[...]
    amount = wt[...]
    first = amount.astype(jnp.bfloat16)
    left = amount - first.astype(jnp.float32)
    second = left.astype(jnp.bfloat16)
    third = (left - second.astype(jnp.float32)).astype(jnp.bfloat16)
    line = lax.broadcasted_iota(jnp.int32, (depth * rows, entries), 0) == cell // width
    lane_hit = lax.broadcasted_iota(jnp.int32, (width, entries), 0) == lax.rem(cell, width)
    line = jnp.where(line, 1.0, 0.0).astype(jnp.bfloat16)
    total = jnp.zeros((depth * rows, width), jnp.float32)
    for part in (third, second, first):
        spread = jnp.where(lane_hit, part.astype(jnp.float32), 0.0).astype(jnp.bfloat16)
        total = total + lax.dot_general(
            line, spread, (((1,), (1,)), ((), ())), preferred_element_type=jnp.float32
        )
    for z in range(depth):
        wgrid[z] = total[z * rows : (z + 1) * rows]

    loads[2].wait()

    def field(k, c, z):
        return sv[k, c, z].astype(jnp.float32)

    for k in range(steps):
        acc = jnp.zeros((rows, width), jnp.float32)
        for z in range(depth):
            square = jnp.zeros((rows, width), jnp.float32)
            for c in range(comps):
                f = field(k, c, z)
                square = square + f * f
            acc = acc + wgrid[z] * square
        pw_out[k : k + 1, :] = jnp.sum(acc, 0, keepdims=True)

    greeted = (n_lat - 1) + (n_ha - 1) * (1 + lat_dn.astype(jnp.int32) + lat_up.astype(jnp.int32))
    pl.semaphore_wait(barrier, greeted)

    over_ha = [
        exchange(pw_out, pw_ha.at[d - 1], (lat, lax.rem(ha + d, n_ha))) for d in range(1, n_ha)
    ]

    loads[3].wait()
    loads[4].wait()

    def material(z):
        label = lb[z]
        eps = jnp.full((rows, width), eps_table[0], jnp.float32)
        chi = jnp.full((rows, width), 3.0 * chi_table[0], jnp.float32)
        for region in range(1, regions):
            member = label == region
            eps = jnp.where(member, eps_table[region], eps)
            chi = jnp.where(member, 3.0 * chi_table[region], chi)
        return eps, chi

    last = steps - 1
    for z in reversed(range(depth)):
        eps, chi = material(z)
        for c in range(comps):
            f = field(last, c, z)
            inverse = 1.0 / (eps + chi * f * f)
            plain = e[c, z] * inverse
            driven = wgrid[z] * f * inverse
            ab[0, c, z] = plain
            ab[1, c, z] = driven
            if c > 0:
                slot = (c - 1) * depth + z
                rab_out[slot : slot + 1, :] = plain[rows - 1 : rows]
                slot = slot + 2 * depth
                rab_out[slot : slot + 1, :] = driven[rows - 1 : rows]

    zab_in = exchange(ab.at[:, pl.ds(0, 2), depth - 1], zab, (lat, ha_next), ha_up, ha_dn)
    rab_in = exchange(rab_out, rab, (lat_next, ha), lat_up, lat_dn)

    for arrive in over_ha:
        arrive()
    power_rows = pw_out[...]
    for d in range(1, n_ha):
        power_rows = power_rows + pw_ha[d - 1]
    pw_sum[...] = power_rows
    over_lat = [
        exchange(pw_sum, pw_lat.at[d - 1], (lax.rem(lat + d, n_lat), ha)) for d in range(1, n_lat)
    ]

    loads[5].wait()
    dens_lo_in = exchange(
        dens.at[pl.ds(rows - 2 * RADIUS, 2 * RADIUS)], dens_lo, (lat_next, ha), lat_up, lat_dn
    )
    dens_hi_in = exchange(
        dens.at[pl.ds(0, 2 * RADIUS)], dens_hi, (lat_prev, ha), lat_dn, lat_up
    )

    for k in range(last):
        for z in range(depth):
            eps, chi = material(z)
            for c in range(comps):
                f = field(k, c, z)
                rinv[k, c, z] = 1.0 / (eps + chi * f * f)

    for arrive in over_lat:
        arrive()
    for d in range(1, n_lat):
        power_rows = power_rows + pw_lat[d - 1]
    count_all = entries * n_lat * n_ha
    power = jnp.sum(power_rows, 1, keepdims=True) / count_all + epsilon
    inverse_power = 1.0 / power

    lane = lax.broadcasted_iota(jnp.int32, (rows, width), 1)
    row = lax.broadcasted_iota(jnp.int32, (rows, width), 0)

    def y_lower(v):
        return jnp.where(lane == 0, 0.0, pltpu.roll(v, 1, 1))

    def y_upper(v):
        return jnp.where(lane == width - 1, 0.0, pltpu.roll(v, width - 1, 1))

    def x_lower(v, edge):
        return jnp.where(row == 0, edge, pltpu.roll(v, 1, 0))

    def x_upper(v, edge):
        return jnp.where(row == rows - 1, edge, pltpu.roll(v, rows - 1, 0))

    def add_plane(k, z, values, acc):
        inner = jnp.zeros((rows, width), jnp.float32)
        for c in range(comps):
            inner = inner + values[c] * field(k, c, z)
        return acc + jnp.where(lb[z] == 0, inner, 0.0)

    acc = jnp.zeros((rows, width), jnp.float32)
    h_prev = h0
    for k in reversed(range(steps)):
        gain = inverse_power[k : k + 1, :]
        if k == last:
            for z in range(depth):
                values = [ab[0, c, z] + gain * ab[1, c, z] for c in range(comps)]
                for c in range(comps):
                    s[k, c, z] = values[c]
                acc = add_plane(k, z, values, acc)
            rab_in()
            low_rows = rab[pl.ds(0, 2 * depth), :] + gain * rab[pl.ds(2 * depth, 2 * depth), :]
            loads[6].wait()
        else:
            rl_in()
            low_rows = rl[k]

        def lower_layer(z, below_x, below_y):
            sx, sy, sz = s[k, 0, z], s[k, 1, z], s[k, 2, z]
            edge_y = low_rows[z : z + 1]
            edge_z = low_rows[depth + z : depth + z + 1]
            curl_x = sz - y_lower(sz) - (sy - below_y)
            curl_y = sx - below_x - (sz - x_lower(sz, edge_z))
            curl_z = sy - x_lower(sy, edge_y) - (sx - y_lower(sx))
            new = (
                h_prev_at(0, z) - time_step * curl_x,
                h_prev_at(1, z) - time_step * curl_y,
                h_prev_at(2, z) - time_step * curl_z,
            )
            for c in range(comps):
                hh[k, c, z] = new[c]
            ru_out[k, z : z + 1, :] = new[1][0:1]
            ru_out[k, depth + z : depth + z + 1, :] = new[2][0:1]

        def h_prev_at(c, z):
            return h0[c, z] if k == last else hh[k + 1, c, z]

        for z in range(1, depth):
            lower_layer(z, s[k, 0, z - 1], s[k, 1, z - 1])
        if k == last:
            zab_in()
            lower_layer(0, zab[0, 0] + gain * zab[1, 0], zab[0, 1] + gain * zab[1, 1])
        else:
            zl_in()
            lower_layer(0, zl[k, 0], zl[k, 1])

        zu_in = exchange(hh.at[k, pl.ds(0, 2), 0], zu.at[k], (lat, ha_prev), ha_dn, ha_up)
        ru_in = exchange(ru_out.at[k], ru.at[k], (lat_prev, ha), lat_dn, lat_up)

        if k == last:
            dens_lo_in()
            dens_hi_in()
            extended = jnp.concatenate([dens_lo[...], dens[...], dens_hi[...]], 0)
            filtered = filter_rows(extended, rows + 2 * RADIUS)
            slope = jnp.tanh(sharpness * (filtered - threshold))
            deriv[...] = (
                sharpness
                * (1.0 - slope * slope)
                / (jnp.tanh(sharpness * threshold) + jnp.tanh(sharpness * (1.0 - threshold)))
            )
        if k == 0:
            store_h = pltpu.make_async_copy(hh.at[0], out_h, local_sem.at[len(loads)])
            store_h.start()
            for arrive in plane_in:
                arrive()
            middle = plane[...]
            head = plane_lo[0]
            tail = plane_hi[0]
            for d in range(1, n_ha):
                middle = middle + plane_ha[d - 1]
                head = head + plane_lo[d]
                tail = tail + plane_hi[d]
            product = jnp.concatenate([head, middle, tail], 0) * deriv[...]
            grad[...] = filter_rows(product, rows)
            store_g = pltpu.make_async_copy(grad, out_g, local_sem.at[len(loads) + 1])
            store_g.start()

        ru_in()
        high_rows = ru[k]

        def upper_layer(z, above_x, above_y):
            hx, hy, hz = hh[k, 0, z], hh[k, 1, z], hh[k, 2, z]
            edge_y = high_rows[z : z + 1]
            edge_z = high_rows[depth + z : depth + z + 1]
            curl_x = y_upper(hz) - hz - (above_y - hy)
            curl_y = above_x - hx - (x_upper(hz, edge_z) - hz)
            curl_z = x_upper(hy, edge_y) - hy - (y_upper(hx) - hx)
            curl = (curl_x, curl_y, curl_z)
            values = []
            for c in range(comps):
                now = e[c, z] + time_step * curl[c]
                if k == last:
                    now = now + gain * (wgrid[z] * field(k, c, z))
                if k > 0:
                    after = inverse_power[k - 1 : k, :]
                    now = now + after * (wgrid[z] * field(k - 1, c, z))
                    value = now * rinv[k - 1, c, z]
                    s[k - 1, c, z] = value
                    values.append(value)
                    if c > 0:
                        slot = (c - 1) * depth + z
                        rl_out[k - 1, slot : slot + 1, :] = value[rows - 1 : rows]
                e[c, z] = now
            return values

        for z in range(depth):
            if z == depth - 1:
                zu_in()
                values = upper_layer(z, zu[k, 0], zu[k, 1])
            else:
                values = upper_layer(z, hh[k, 0, z + 1], hh[k, 1, z + 1])
            if k > 0:
                acc = add_plane(k - 1, z, values, acc)

        if k > 0:
            zl_in = exchange(
                s.at[k - 1, pl.ds(0, 2), depth - 1], zl.at[k - 1], (lat, ha_next), ha_up, ha_dn
            )
            rl_in = exchange(rl_out.at[k - 1], rl.at[k - 1], (lat_next, ha), lat_up, lat_dn)
        if k == 1:
            plane[...] = acc
            plane_in = []
            for d in range(n_ha):
                other = lax.rem(ha + d, n_ha)
                if d > 0:
                    plane_in.append(exchange(plane, plane_ha.at[d - 1], (lat, other)))
                plane_in.append(
                    exchange(
                        plane.at[pl.ds(rows - RADIUS, RADIUS)],
                        plane_lo.at[d],
                        (lat_next, other),
                        lat_up,
                        lat_dn,
                    )
                )
                plane_in.append(
                    exchange(
                        plane.at[pl.ds(0, RADIUS)],
                        plane_hi.at[d],
                        (lat_prev, other),
                        lat_dn,
                        lat_up,
                    )
                )

    store_e = pltpu.make_async_copy(e, out_e, local_sem.at[len(loads) + 2])
    store_e.start()
    for finish in issued:
        finish()
    store_h.wait()
    store_g.wait()
    store_e.wait()


def body(
    adjoint_e, adjoint_h, saved_e, labels, eps_table, chi_table, density, mon_cells, mon_weight
):
    n_lat, n_ha = lax.axis_size("lat"), lax.axis_size("ha")
    steps, comps, depth, rows, width = saved_e.shape
    entries = mon_cells.shape[0]
    f32 = jnp.float32
    block = (comps, depth, rows, width)
    copies = (n_ha - 1) + (n_lat - 1) + 4 + 4 * steps - 2 + 3 * n_ha - 1
    anywhere = pl.BlockSpec(memory_space=pl.ANY)
    scalars = pl.BlockSpec(memory_space=pltpu.SMEM)
    scratch = [
        pltpu.VMEM(block, f32),
        pltpu.VMEM(block, f32),
        pltpu.VMEM(saved_e.shape, saved_e.dtype),
        pltpu.VMEM(labels.shape, labels.dtype),
        pltpu.VMEM((rows, width), f32),
        pltpu.VMEM((1, entries), mon_cells.dtype),
        pltpu.VMEM((1, entries), f32),
        pltpu.VMEM((depth, rows, width), f32),
        pltpu.VMEM((2,) + block, f32),
        pltpu.VMEM((steps,) + block, f32),
        pltpu.VMEM((steps,) + block, f32),
        pltpu.VMEM((max(steps - 1, 1),) + block, f32),
        pltpu.VMEM((rows, width), f32),
        pltpu.VMEM((rows, width), f32),
        pltpu.VMEM((2 * RADIUS, width), f32),
        pltpu.VMEM((2 * RADIUS, width), f32),
        pltpu.VMEM((rows + 2 * RADIUS, width), f32),
        pltpu.VMEM((2, 2, rows, width), f32),
        pltpu.VMEM((4 * depth, width), f32),
        pltpu.VMEM((4 * depth, width), f32),
        pltpu.VMEM((steps, 2, rows, width), f32),
        pltpu.VMEM((steps, 2 * depth, width), f32),
        pltpu.VMEM((steps, 2 * depth, width), f32),
        pltpu.VMEM((steps, 2, rows, width), f32),
        pltpu.VMEM((steps, 2 * depth, width), f32),
        pltpu.VMEM((steps, 2 * depth, width), f32),
        pltpu.VMEM((steps, width), f32),
        pltpu.VMEM((max(n_ha - 1, 1), steps, width), f32),
        pltpu.VMEM((steps, width), f32),
        pltpu.VMEM((max(n_lat - 1, 1), steps, width), f32),
        pltpu.VMEM((max(n_ha - 1, 1), rows, width), f32),
        pltpu.VMEM((n_ha, RADIUS, width), f32),
        pltpu.VMEM((n_ha, RADIUS, width), f32),
        pltpu.SemaphoreType.DMA((10,)),
        pltpu.SemaphoreType.DMA((copies,)),
        pltpu.SemaphoreType.DMA((copies,)),
    ]
    return pl.pallas_call(
        functools.partial(kernel, n_lat, n_ha),
        out_shape=(
            jax.ShapeDtypeStruct(block, f32),
            jax.ShapeDtypeStruct(block, f32),
            jax.ShapeDtypeStruct((rows, width), f32),
        ),
        in_specs=[anywhere] * 4 + [scalars] * 2 + [anywhere] * 3,
        out_specs=(anywhere, anywhere, anywhere),
        scratch_shapes=scratch,
        compiler_params=pltpu.CompilerParams(
            collective_id=0, has_side_effects=True, vmem_limit_bytes=40 * 2**20
        ),
    )(
        adjoint_e,
        adjoint_h,
        saved_e,
        labels,
        eps_table,
        chi_table,
        density,
        mon_cells.reshape(1, entries),
        mon_weight.reshape(1, entries),
    )


def solution(mesh):
    return jax.shard_map(
        body,
        mesh=mesh,
        in_specs=(
            P(None, "ha", "lat", None),
            P(None, "ha", "lat", None),
            P(None, None, "ha", "lat", None),
            P("ha", "lat", None),
            P(),
            P(),
            P("lat", None),
            P(("lat", "ha")),
            P(("lat", "ha")),
        ),
        out_specs=(P(None, "ha", "lat", None), P(None, "ha", "lat", None), P("lat", None)),
        check_vma=False,
    )
```

time: 223 us -> 34 us (0.15)
  local copies, waits for them, and re-layouts: 83.8 us -> 8.1 us
  blocking collectives: 49.3 us -> 0 us
  other arithmetic: 42.8 us -> 0 us
  starting transfers between devices: 28.3 us -> 0 us
  Pallas kernels: 0 us -> 24.8 us
  waiting for transfers between devices: 11.2 us -> 0 us
  matrix products: 2.8 us -> 0 us
    psum x2 -> x0, blocking collectives: 49.3 us -> none  [the longest x1 42.3 us: body(): power = lax.psum(term, ('lat', 'ha')) / count_all + epsilon]
    scatter-add x2 -> x0, other arithmetic: 29.4 us -> none  [body(): lam_e.reshape(3, -1).at[:, mon_cells].add(mon_weight * picked / power)]
    ppermute x12 -> x0, starting transfers between devices: 28.3 us -> none  [the longest x8 21.1 us: passed_along(): lax.ppermute(value, axis, [(source, source + steps) for source in range(f...]
    pallas_call x0 -> x1, Pallas kernels: none -> 24.8 us  [body(): pl.pallas_call(functools.partial(kernel, n_lat, n_ha), out_shape=(jax.Sha...]
    reshape x2 -> x0, local copies, waits for them, and re-layouts: 20 us -> none  [body(): lam_e.reshape(3, -1).at[:, mon_cells].add(mon_weight * picked / power)]
    scatter-add x2 -> x0, local copies, waits for them, and re-layouts: 18.9 us -> none  [body(): lam_e.reshape(3, -1).at[:, mon_cells].add(mon_weight * picked / power)]
    another operation x4 -> x0, local copies, waits for them, and re-layouts: 11.7 us -> none  [body(): picked = saved_e[index].reshape(3, -1)[:, mon_cells].astype(jnp.float32)]
    ppermute x12 -> x0, waiting for transfers between devices: 11.2 us -> none  [the longest x8 11.2 us: passed_along(): lax.ppermute(value, axis, [(source, source + steps) for source in range(f...]
  transfers between devices with their start and end apart: 12 -> 0, of which waited for: 5 -> 0; matrix products, arithmetic and copies ran while one was open for 6% -> 0% of each run, Pallas kernels for 0% -> 0%
where the time goes in v1:
time: 34 us; the launch traced here: 33.6 us
  Pallas kernels  24.8 us (73%)
  local copies, waits for them, and re-layouts  8.1 us (24%)
  between operations  0.67 us (2%)
    pallas_call x1, Pallas kernels, body(): pl.pallas_call(functools.partial(kernel, n_lat, n_ha), out_shape=(jax.Sha...  24.8 us
    unnamed x21, local copies, waits for them, and re-layouts  8.1 us

profile of v1, /device:TPU:0, one launch (start us, length us, event | category | flops | bytes accessed | tf_op | source)
XLA Modules:
  0.0 33.6 jit_solution(11487928776097526773)
XLA Ops:
  0.6 0.0 copy-start.5
  0.6 0.0 copy-start.7
  0.7 0.0 copy-start.8
  0.7 0.7 %copy-done.5 = s32[512]{0:T(512)S(1)} copy-done((s32[512]{0:T(512)S(1)}, s32[512]{0:T(512)}, u32[]{:S(2)}) %copy-start.5) | copy-done | bytes 2072
  1.3 0.0 copy-done.7
  1.3 0.0 copy-done.8
  1.3 0.0 copy-start
  1.3 1.0 %copy-done = f32[3,4,64,128]{3,2,1,0:T(8,128)S(1)} copy-done((f32[3,4,64,128]{3,2,1,0:T(8,128)S(1)}, f32[3,4,64,128]{3,2,1,0:T(8,128)}, u32[]{:S(2)}) %copy-start) | copy-done | bytes 393240
  2.3 0.0 copy-start.1
  2.3 1.0 %copy-done.1 = f32[3,4,64,128]{3,2,1,0:T(8,128)S(1)} copy-done((f32[3,4,64,128]{3,2,1,0:T(8,128)S(1)}, f32[3,4,64,128]{3,2,1,0:T(8,128)}, u32[]{:S(2)}) %copy-start.1) | copy-done | bytes 393240
  3.3 0.0 copy-start.2
  3.3 1.0 %copy-done.2 = bf16[2,3,4,64,128]{4,3,2,1,0:T(8,128)(2,1)S(1)} copy-done((bf16[2,3,4,64,128]{4,3,2,1,0:T(8,128)(2,1)S(1)}, bf16[2,3,4,64,128]{4,3,2,1,0:T(8,128)(2,1)}, u32[]{:S(2)}) %copy-start.2) | copy-done | bytes 393240
  4.3 0.0 copy-start.3
  4.3 0.9 %copy-done.3 = s32[4,64,128]{2,1,0:T(8,128)S(1)} copy-done((s32[4,64,128]{2,1,0:T(8,128)S(1)}, s32[4,64,128]{2,1,0:T(8,128)}, u32[]{:S(2)}) %copy-start.3) | copy-done | bytes 131096
  5.2 0.0 copy-start.4
  5.2 0.8 %copy-done.4 = f32[64,128]{1,0:T(8,128)S(1)} copy-done((f32[64,128]{1,0:T(8,128)S(1)}, f32[64,128]{1,0:T(8,128)}, u32[]{:S(2)}) %copy-start.4) | copy-done | bytes 32792
  6.0 0.0 copy-start.6
  6.0 0.7 %copy-done.6 = f32[512]{0:T(512)S(1)} copy-done((f32[512]{0:T(512)S(1)}, f32[512]{0:T(512)}, u32[]{:S(2)}) %copy-start.6) | copy-done | bytes 2072
  6.7 24.8 %shard_map.112 = (f32[3,4,64,128]{3,2,1,0:T(8,128)S(1)}, f32[3,4,64,128]{3,2,1,0:T(8,128)S(1)}, f32[64,128]{1,0:T(8,128)S(1)}) custom-call(f32[3,4,64,128]{3,2,1,0:T(8,128)S(1)} %copy-done, f32[3,4,64,128]{3,2,1,0:T(8,128)S(1)} %copy-done.1, bf16[2,3,4,64,128]{4,3,2,1,0:T(8,128)(2,1)S(1)} %copy-done.2, s32[4,64,128]{2,1,0:T(8,128)S(1)} %copy-done.3, ...), custom_call_target="tpu_custom_call" | custom-call | tf_op jit(solution)/shard_map/pallas_call | solution.py:494
  31.5 0.7 %copy.15 = f32[3,4,64,128]{3,2,1,0:T(8,128)} copy(f32[3,4,64,128]{3,2,1,0:T(8,128)S(1)} %get-tuple-element.6) | data formatting | bytes 786432
  32.2 0.7 %copy.16 = f32[3,4,64,128]{3,2,1,0:T(8,128)} copy(f32[3,4,64,128]{3,2,1,0:T(8,128)S(1)} %get-tuple-element.7) | data formatting | bytes 786432
  33.0 0.6 %copy.17 = f32[64,128]{1,0:T(8,128)} copy(f32[64,128]{1,0:T(8,128)S(1)} %get-tuple-element.8) | data formatting | bytes 65536
Async XLA Ops:
  0.6 0.7 %copy-start.5 = (s32[512]{0:T(512)S(1)}, s32[512]{0:T(512)}, u32[]{:S(2)}) copy-start(s32[512]{0:T(512)} %param.16) | copy-start | bytes 6148
  0.6 0.7 %copy-start.7 = (f32[4]{0:T(128)S(1)}, f32[4]{0:T(128)}, u32[]{:S(2)}) copy-start(f32[4]{0:T(128)} %eps_table.1) | copy-start | bytes 52
  0.7 0.7 %copy-start.8 = (f32[4]{0:T(128)S(1)}, f32[4]{0:T(128)}, u32[]{:S(2)}) copy-start(f32[4]{0:T(128)} %chi_table.1) | copy-start | bytes 52
  1.3 1.0 %copy-start = (f32[3,4,64,128]{3,2,1,0:T(8,128)S(1)}, f32[3,4,64,128]{3,2,1,0:T(8,128)}, u32[]{:S(2)}) copy-start(f32[3,4,64,128]{3,2,1,0:T(8,128)} %adj_e.1) | copy-start | bytes 1179652
  2.3 1.0 %copy-start.1 = (f32[3,4,64,128]{3,2,1,0:T(8,128)S(1)}, f32[3,4,64,128]{3,2,1,0:T(8,128)}, u32[]{:S(2)}) copy-start(f32[3,4,64,128]{3,2,1,0:T(8,128)} %adj_h.1) | copy-start | bytes 1179652
  3.3 1.0 %copy-start.2 = (bf16[2,3,4,64,128]{4,3,2,1,0:T(8,128)(2,1)S(1)}, bf16[2,3,4,64,128]{4,3,2,1,0:T(8,128)(2,1)}, u32[]{:S(2)}) copy-start(bf16[2,3,4,64,128]{4,3,2,1,0:T(8,128)(2,1)} %saved.1) | copy-start | bytes 1179652
  4.3 0.9 %copy-start.3 = (s32[4,64,128]{2,1,0:T(8,128)S(1)}, s32[4,64,128]{2,1,0:T(8,128)}, u32[]{:S(2)}) copy-start(s32[4,64,128]{2,1,0:T(8,128)} %labels.1) | copy-start | bytes 393220
  5.2 0.8 %copy-start.4 = (f32[64,128]{1,0:T(8,128)S(1)}, f32[64,128]{1,0:T(8,128)}, u32[]{:S(2)}) copy-start(f32[64,128]{1,0:T(8,128)} %density.1) | copy-start | bytes 98308
  6.0 0.7 %copy-start.6 = (f32[512]{0:T(512)S(1)}, f32[512]{0:T(512)}, u32[]{:S(2)}) copy-start(f32[512]{0:T(512)} %param.17) | copy-start | bytes 6148

commit v2 on v1

v2 whole, which is shorter than its diff:
```python
import functools

import jax
import jax.numpy as jnp
from jax import lax
from jax.experimental import pallas as pl
from jax.experimental.pallas import tpu as pltpu
from jax.sharding import PartitionSpec as P

RADIUS = 16

sharpness = 8.0
threshold = 0.5
time_step = 0.5
epsilon = 1e-05

MESH = pl.DeviceIdType.MESH


def cone(offset):
    return jnp.maximum(RADIUS + 1 - jnp.abs(offset), 0).astype(jnp.float32) / (RADIUS + 1) ** 2


def filter_rows(padded, rows):
    width = padded.shape[1]
    i = lax.broadcasted_iota(jnp.int32, (width, width), 0)
    j = lax.broadcasted_iota(jnp.int32, (width, width), 1)
    smoothed = jnp.dot(
        padded, cone(i - j), precision=lax.Precision.HIGHEST, preferred_element_type=jnp.float32
    )
    row_out = lax.broadcasted_iota(jnp.int32, (rows, rows + 2 * RADIUS), 0)
    row_in = lax.broadcasted_iota(jnp.int32, (rows, rows + 2 * RADIUS), 1)
    return jnp.dot(
        cone(row_in - RADIUS - row_out),
        smoothed,
        precision=lax.Precision.HIGHEST,
        preferred_element_type=jnp.float32,
    )


def kernel(
    n_lat,
    n_ha,
    adj_e,
    adj_h,
    saved,
    labels,
    eps_table,
    chi_table,
    density,
    cells,
    weight,
    out_e,
    out_h,
    out_g,
    e,
    h0,
    sv,
    lb,
    dens,
    cl,
    wt,
    wgrid,
    s,
    hh,
    rinv,
    plane,
    dens_lo,
    dens_hi,
    deriv,
    hz,
    hr_out,
    hr,
    zl,
    zu,
    rl_out,
    rl,
    ru_out,
    ru,
    ca_out,
    ca,
    cb_out,
    cb,
    pw_out,
    pw_in,
    plane_ha,
    plane_lo,
    plane_hi,
    local_sem,
    send_sem,
    recv_sem,
):
    steps, comps, depth, rows, width = sv.shape
    regions = eps_table.shape[0]
    entries = cl.shape[1]
    last = steps - 1
    devices = n_lat * n_ha
    lat = lax.axis_index("lat")
    ha = lax.axis_index("ha")
    lat_dn, lat_up = lat > 0, lat < n_lat - 1
    ha_dn, ha_up = ha > 0, ha < n_ha - 1
    lat_prev, lat_next = jnp.maximum(lat - 1, 0), jnp.minimum(lat + 1, n_lat - 1)
    ha_prev, ha_next = jnp.maximum(ha - 1, 0), jnp.minimum(ha + 1, n_ha - 1)

    pairs = [
        (cells, cl),
        (weight, wt),
        (saved, sv),
        (labels, lb),
        (adj_h, h0),
        (adj_e, e),
        (density, dens),
    ]
    loads = [pltpu.make_async_copy(a, b, local_sem.at[i]) for i, (a, b) in enumerate(pairs)]
    for load in loads:
        load.start()

    barrier = pltpu.get_barrier_semaphore()

    def peer(d):
        there = lax.rem(lat * n_ha + ha + d, devices)
        return (lax.div(there, n_ha), lax.rem(there, n_ha))

    for d in range(1, devices):
        pl.semaphore_signal(barrier, inc=1, device_id=peer(d), device_id_type=MESH)

    issued = []

    def exchange(src, dst, target, sends=None, receives=None):
        index = len(issued)

        def copy():
            return pltpu.make_async_remote_copy(
                src_ref=src,
                dst_ref=dst,
                send_sem=send_sem.at[index],
                recv_sem=recv_sem.at[index],
                device_id=target,
                device_id_type=MESH,
            )

        def guarded(condition, action):
            if condition is None:
                action()
            else:
                pl.when(condition)(action)

        issued.append(lambda: guarded(sends, lambda: copy().wait_send()))
        guarded(sends, lambda: copy().start())

        def arrive():
            guarded(receives, lambda: copy().wait_recv())
            if receives is not None:

                @pl.when(jnp.logical_not(receives))
                def _():
                    dst[...] = jnp.zeros(dst.shape, dst.dtype)

        return arrive

    loads[0].wait()
    loads[1].wait()
    cell = cl[...]
    amount = wt[...]
    first = amount.astype(jnp.bfloat16)
    left = amount - first.astype(jnp.float32)
    second = left.astype(jnp.bfloat16)
    third = (left - second.astype(jnp.float32)).astype(jnp.bfloat16)
    line = lax.broadcasted_iota(jnp.int32, (depth * rows, entries), 0) == cell // width
    lane_hit = lax.broadcasted_iota(jnp.int32, (width, entries), 0) == lax.rem(cell, width)
    line = jnp.where(line, 1.0, 0.0).astype(jnp.bfloat16)
    total = jnp.zeros((depth * rows, width), jnp.float32)
    for part in (third, second, first):
        spread = jnp.where(lane_hit, part.astype(jnp.float32), 0.0).astype(jnp.bfloat16)
        total = total + lax.dot_general(
            line, spread, (((1,), (1,)), ((), ())), preferred_element_type=jnp.float32
        )
    for z in range(depth):
        wgrid[z] = total[z * rows : (z + 1) * rows]

    loads[2].wait()

    def field(k, c, z):
        return sv[k, c, z].astype(jnp.float32)

    for k in range(steps):
        acc = jnp.zeros((rows, width), jnp.float32)
        for z in range(depth):
            square = jnp.zeros((rows, width), jnp.float32)
            for c in range(comps):
                f = field(k, c, z)
                square = square + f * f
            acc = acc + wgrid[z] * square
        pw_out[k : k + 1, :] = jnp.sum(acc, 0, keepdims=True)

    pl.semaphore_wait(barrier, devices - 1)
    power_in = [exchange(pw_out, pw_in.at[d - 1], peer(d)) for d in range(1, devices)]

    loads[4].wait()
    for c in range(1, comps):
        for z in range(depth):
            slot = (c - 1) * depth + z
            hr_out[slot : slot + 1, :] = h0[c, z, 0:1]
    hz_in = exchange(h0.at[pl.ds(0, 2), 0], hz.at[steps], (lat, ha_prev), ha_dn, ha_up)
    hr_in = exchange(hr_out, hr.at[steps], (lat_prev, ha), lat_dn, lat_up)
    loads[6].wait()
    dens_lo_in = exchange(
        dens.at[pl.ds(rows - 2 * RADIUS, 2 * RADIUS)], dens_lo, (lat_next, ha), lat_up, lat_dn
    )
    dens_hi_in = exchange(
        dens.at[pl.ds(0, 2 * RADIUS)], dens_hi, (lat_prev, ha), lat_dn, lat_up
    )

    loads[3].wait()
    for z in range(depth):
        label = lb[z]
        eps = jnp.full((rows, width), eps_table[0], jnp.float32)
        chi = jnp.full((rows, width), 3.0 * chi_table[0], jnp.float32)
        for region in range(1, regions):
            member = label == region
            eps = jnp.where(member, eps_table[region], eps)
            chi = jnp.where(member, 3.0 * chi_table[region], chi)
        for k in range(steps):
            for c in range(comps):
                f = field(k, c, z)
                rinv[k, c, z] = 1.0 / (eps + chi * f * f)

    loads[5].wait()
    for arrive in power_in:
        arrive()
    power_rows = pw_out[...]
    for d in range(1, devices):
        power_rows = power_rows + pw_in[d - 1]
    power = jnp.sum(power_rows, 1, keepdims=True) / (entries * devices) + epsilon
    inverse_power = 1.0 / power

    lane = lax.broadcasted_iota(jnp.int32, (rows, width), 1)
    row = lax.broadcasted_iota(jnp.int32, (rows, width), 0)
    lane_few = lax.broadcasted_iota(jnp.int32, (depth, width), 1)
    inside_ha = ha_up.astype(jnp.float32)
    inside_lat = lat_up.astype(jnp.float32)

    def y_lower(v):
        return jnp.where(lane == 0, 0.0, pltpu.roll(v, 1, 1))

    def y_lower_few(v):
        return jnp.where(lane_few == 0, 0.0, pltpu.roll(v, 1, 1))

    def y_upper(v):
        return jnp.where(lane == width - 1, 0.0, pltpu.roll(v, width - 1, 1))

    def x_lower(v, edge):
        return jnp.where(row == 0, edge, pltpu.roll(v, 1, 0))

    def x_upper(v, edge):
        return jnp.where(row == rows - 1, edge, pltpu.roll(v, rows - 1, 0))

    def scale_layer(k, z, fields, acc):
        gain = inverse_power[k : k + 1, :]
        inner = jnp.zeros((rows, width), jnp.float32)
        for c in range(comps):
            f = field(k, c, z)
            now = fields[c] + gain * (wgrid[z] * f)
            value = now * rinv[k, c, z]
            e[c, z] = now
            s[k, c, z] = value
            inner = inner + value * f
            slot = c * depth + z
            ru_out[k, slot : slot + 1, :] = value[0:1]
            if c > 0:
                slot = slot - depth
                rl_out[k, slot : slot + 1, :] = value[rows - 1 : rows]
            if c == 0 and z == depth - 1:
                ca_out[k] = value[0:1]
            if c == 2 and z == 0:
                cb_out[k] = value[rows - 1 : rows]
        return acc + jnp.where(lb[z] == 0, inner, 0.0)

    def send_bottom(k):
        return exchange(s.at[k, :, 0], zu.at[k], (lat, ha_prev), ha_dn, ha_up)

    def send_top(k):
        return exchange(s.at[k, pl.ds(0, 2), depth - 1], zl.at[k], (lat, ha_next), ha_up, ha_dn)

    def send_rows(k):
        return (
            exchange(rl_out.at[k], rl.at[k], (lat_next, ha), lat_up, lat_dn),
            exchange(ru_out.at[k], ru.at[k], (lat_prev, ha), lat_dn, lat_up),
            exchange(
                ca_out.at[k],
                ca.at[k],
                (lat_prev, ha_next),
                jnp.logical_and(lat_dn, ha_up),
                jnp.logical_and(lat_up, ha_dn),
            ),
            exchange(
                cb_out.at[k],
                cb.at[k],
                (lat_next, ha_prev),
                jnp.logical_and(lat_up, ha_dn),
                jnp.logical_and(lat_dn, ha_up),
            ),
        )

    acc = jnp.zeros((rows, width), jnp.float32)
    order = [0] + ([depth - 1] if depth > 1 else []) + list(range(1, depth - 1))
    for z in order:
        acc = scale_layer(last, z, [e[c, z] for c in range(comps)], acc)
        if z == 0:
            zu_in = send_bottom(last)
        if z == depth - 1:
            zl_in = send_top(last)
    rl_in, ru_in, ca_in, cb_in = send_rows(last)

    dens_lo_in()
    dens_hi_in()
    extended = jnp.concatenate([dens_lo[...], dens[...], dens_hi[...]], 0)
    filtered = filter_rows(extended, rows + 2 * RADIUS)
    slope = jnp.tanh(sharpness * (filtered - threshold))
    deriv[...] = (
        sharpness
        * (1.0 - slope * slope)
        / (jnp.tanh(sharpness * threshold) + jnp.tanh(sharpness * (1.0 - threshold)))
    )
    hz_in()
    hr_in()

    for k in reversed(range(steps)):

        def before(c, z):
            return h0[c, z] if k == last else hh[k + 1, c, z]

        def put(c, z, value):
            if k == 0:
                out_h[c, z] = value
            else:
                hh[k, c, z] = value

        def after(c, z):
            return out_h[c, z] if k == 0 else hh[k, c, z]

        def lower_layer(z, below_x, below_y):
            sx, sy, sz = s[k, 0, z], s[k, 1, z], s[k, 2, z]
            edge_y = low_rows[z : z + 1]
            edge_z = low_rows[depth + z : depth + z + 1]
            curl_x = sz - y_lower(sz) - (sy - below_y)
            curl_y = sx - below_x - (sz - x_lower(sz, edge_z))
            curl_z = sy - x_lower(sy, edge_y) - (sx - y_lower(sx))
            put(0, z, before(0, z) - time_step * curl_x)
            put(1, z, before(1, z) - time_step * curl_y)
            put(2, z, before(2, z) - time_step * curl_z)

        rl_in()
        low_rows = rl[k]
        for z in range(1, depth):
            lower_layer(z, s[k, 0, z - 1], s[k, 1, z - 1])

        ru_in()
        ca_in()
        hx_rows = ru[k, pl.ds(0, depth), :]
        hy_rows = ru[k, pl.ds(depth, depth), :]
        hz_rows = ru[k, pl.ds(2 * depth, depth), :]
        own_y = jnp.concatenate([s[k, 1, z, rows - 1 : rows] for z in range(depth)], 0)
        own_z = jnp.concatenate([s[k, 2, z, rows - 1 : rows] for z in range(depth)], 0)
        under = ca[k]
        if depth > 1:
            under = jnp.concatenate([under, hx_rows[0 : depth - 1]], 0)
        old_y = hr[k + 1, pl.ds(0, depth), :]
        old_z = hr[k + 1, pl.ds(depth, depth), :]
        high_y = old_y - time_step * (hx_rows - under - (hz_rows - own_z))
        high_z = old_z - time_step * (hy_rows - own_y - (hx_rows - y_lower_few(hx_rows)))
        high_y = high_y * inside_lat
        high_z = high_z * inside_lat
        hr[k, pl.ds(0, depth), :] = high_y
        hr[k, pl.ds(depth, depth), :] = high_z

        zl_in()
        lower_layer(0, zl[k, 0], zl[k, 1])

        def upper_layer(z, above_x, above_y):
            hx, hy, hv = after(0, z), after(1, z), after(2, z)
            edge_y = high_y[z : z + 1]
            edge_z = high_z[z : z + 1]
            curl_x = y_upper(hv) - hv - (above_y - hy)
            curl_y = above_x - hx - (x_upper(hv, edge_z) - hv)
            curl_z = x_upper(hy, edge_y) - hy - (y_upper(hx) - hx)
            return (
                e[0, z] + time_step * curl_x,
                e[1, z] + time_step * curl_y,
                e[2, z] + time_step * curl_z,
            )

        def finish_layer(z, above_x, above_y, acc):
            fields = upper_layer(z, above_x, above_y)
            if k > 0:
                return scale_layer(k - 1, z, fields, acc)
            for c in range(comps):
                out_e[c, z] = fields[c]
            return acc

        for z in range(depth - 1):
            acc = finish_layer(z, after(0, z + 1), after(1, z + 1), acc)
            if z == 0 and k > 0:
                zu_next = send_bottom(k - 1)

        zu_in()
        cb_in()
        top = depth - 1
        nx, ny, nz = zu[k, 0], zu[k, 1], zu[k, 2]
        above_x = hz[k + 1, 0] - time_step * (nz - y_lower(nz) - (ny - s[k, 1, top]))
        above_y = hz[k + 1, 1] - time_step * (nx - s[k, 0, top] - (nz - x_lower(nz, cb[k])))
        above_x = above_x * inside_ha
        above_y = above_y * inside_ha
        hz[k, 0] = above_x
        hz[k, 1] = above_y
        acc = finish_layer(top, above_x, above_y, acc)

        if k > 0:
            if depth == 1:
                zu_next = send_bottom(k - 1)
            zu_in = zu_next
            zl_in = send_top(k - 1)
            rl_in, ru_in, ca_in, cb_in = send_rows(k - 1)
        if k == min(1, last):
            plane[...] = acc
            plane_in = []
            for d in range(n_ha):
                other = lax.rem(ha + d, n_ha)
                if d > 0:
                    plane_in.append(exchange(plane, plane_ha.at[d - 1], (lat, other)))
                plane_in.append(
                    exchange(
                        plane.at[pl.ds(rows - RADIUS, RADIUS)],
                        plane_lo.at[d],
                        (lat_next, other),
                        lat_up,
                        lat_dn,
                    )
                )
                plane_in.append(
                    exchange(
                        plane.at[pl.ds(0, RADIUS)],
                        plane_hi.at[d],
                        (lat_prev, other),
                        lat_dn,
                        lat_up,
                    )
                )

    for arrive in plane_in:
        arrive()
    middle = plane[...]
    low = plane_lo[0]
    high = plane_hi[0]
    for d in range(1, n_ha):
        middle = middle + plane_ha[d - 1]
        low = low + plane_lo[d]
        high = high + plane_hi[d]
    product = jnp.concatenate([low, middle, high], 0) * deriv[...]
    out_g[...] = filter_rows(product, rows)
    for finish in issued:
        finish()


def store(e, h, g, out_e, out_h, out_g, sem):
    copies = [
        pltpu.make_async_copy(e, out_e, sem.at[0]),
        pltpu.make_async_copy(h, out_h, sem.at[1]),
        pltpu.make_async_copy(g, out_g, sem.at[2]),
    ]
    for copy in copies:
        copy.start()
    for copy in copies:
        copy.wait()


def body(
    adjoint_e, adjoint_h, saved_e, labels, eps_table, chi_table, density, mon_cells, mon_weight
):
    n_lat, n_ha = lax.axis_size("lat"), lax.axis_size("ha")
    steps, comps, depth, rows, width = saved_e.shape
    entries = mon_cells.shape[0]
    f32 = jnp.float32
    block = (comps, depth, rows, width)
    copies = (n_lat * n_ha - 1) + 4 + 6 * steps + 3 * n_ha - 1
    vmem = pl.BlockSpec(memory_space=pltpu.VMEM)
    hbm = pl.BlockSpec(memory_space=pltpu.HBM)
    scalars = pl.BlockSpec(memory_space=pltpu.SMEM)
    scratch = [
        pltpu.VMEM(block, f32),
        pltpu.VMEM(block, f32),
        pltpu.VMEM(saved_e.shape, saved_e.dtype),
        pltpu.VMEM(labels.shape, labels.dtype),
        pltpu.VMEM((rows, width), f32),
        pltpu.VMEM((1, entries), mon_cells.dtype),
        pltpu.VMEM((1, entries), f32),
        pltpu.VMEM((depth, rows, width), f32),
        pltpu.VMEM((steps,) + block, f32),
        pltpu.VMEM((steps,) + block, f32),
        pltpu.VMEM((steps,) + block, f32),
        pltpu.VMEM((rows, width), f32),
        pltpu.VMEM((2 * RADIUS, width), f32),
        pltpu.VMEM((2 * RADIUS, width), f32),
        pltpu.VMEM((rows + 2 * RADIUS, width), f32),
        pltpu.VMEM((steps + 1, 2, rows, width), f32),
        pltpu.VMEM((2 * depth, width), f32),
        pltpu.VMEM((steps + 1, 2 * depth, width), f32),
        pltpu.VMEM((steps, 2, rows, width), f32),
        pltpu.VMEM((steps, 3, rows, width), f32),
        pltpu.VMEM((steps, 2 * depth, width), f32),
        pltpu.VMEM((steps, 2 * depth, width), f32),
        pltpu.VMEM((steps, 3 * depth, width), f32),
        pltpu.VMEM((steps, 3 * depth, width), f32),
        pltpu.VMEM((steps, 1, width), f32),
        pltpu.VMEM((steps, 1, width), f32),
        pltpu.VMEM((steps, 1, width), f32),
        pltpu.VMEM((steps, 1, width), f32),
        pltpu.VMEM((steps, width), f32),
        pltpu.VMEM((n_lat * n_ha - 1, steps, width), f32),
        pltpu.VMEM((max(n_ha - 1, 1), rows, width), f32),
        pltpu.VMEM((n_ha, RADIUS, width), f32),
        pltpu.VMEM((n_ha, RADIUS, width), f32),
        pltpu.SemaphoreType.DMA((7,)),
        pltpu.SemaphoreType.DMA((copies,)),
        pltpu.SemaphoreType.DMA((copies,)),
    ]
    results = pl.pallas_call(
        functools.partial(kernel, n_lat, n_ha),
        out_shape=(
            pltpu.VMEM(block, f32),
            pltpu.VMEM(block, f32),
            pltpu.VMEM((rows, width), f32),
        ),
        in_specs=[hbm] * 4 + [scalars] * 2 + [hbm] * 3,
        out_specs=(vmem, vmem, vmem),
        scratch_shapes=scratch,
        compiler_params=pltpu.CompilerParams(
            collective_id=0, has_side_effects=True, vmem_limit_bytes=63 * 2**20
        ),
    )(
        adjoint_e,
        adjoint_h,
        saved_e,
        labels,
        eps_table,
        chi_table,
        density,
        mon_cells.reshape(1, entries),
        mon_weight.reshape(1, entries),
    )
    return pl.pallas_call(
        store,
        out_shape=(
            jax.ShapeDtypeStruct(block, f32),
            jax.ShapeDtypeStruct(block, f32),
            jax.ShapeDtypeStruct((rows, width), f32),
        ),
        in_specs=[vmem] * 3,
        out_specs=(hbm, hbm, hbm),
        scratch_shapes=[pltpu.SemaphoreType.DMA((3,))],
    )(*results)


def solution(mesh):
    return jax.shard_map(
        body,
        mesh=mesh,
        in_specs=(
            P(None, "ha", "lat", None),
            P(None, "ha", "lat", None),
            P(None, None, "ha", "lat", None),
            P("ha", "lat", None),
            P(),
            P(),
            P("lat", None),
            P(("lat", "ha")),
            P(("lat", "ha")),
        ),
        out_specs=(P(None, "ha", "lat", None), P(None, "ha", "lat", None), P("lat", None)),
        check_vma=False,
    )
```

time: 34 us -> 26 us (0.76)
  local copies, waits for them, and re-layouts: 8.1 us -> 2.09 us
  Pallas kernels: 24.8 us -> 23 us
    unnamed x21 -> x6, local copies, waits for them, and re-layouts: 8.1 us -> 2.09 us
    pallas_call x1 -> x2, Pallas kernels: 24.8 us -> 23 us  [the longest x1 21 us: body(): pl.pallas_call(functools.partial(kernel, n_lat, n_ha), out_shape=(pltpu.V...]
where the time goes in v2:
time: 26 us; the launch traced here: 25.8 us
  Pallas kernels  23 us (88%)
  local copies, waits for them, and re-layouts  2.09 us (8%)
  between operations  0.65 us (2%)
    pallas_call x1, Pallas kernels, body(): pl.pallas_call(functools.partial(kernel, n_lat, n_ha), out_shape=(pltpu.V...  21 us
    unnamed x6, local copies, waits for them, and re-layouts  2.09 us
    pallas_call x1, Pallas kernels, body(): pl.pallas_call(store, out_shape=(jax.ShapeDtypeStruct(block, f32), jax.Sh...  2.02 us

profile of v2, /device:TPU:0, one launch (start us, length us, event | category | flops | bytes accessed | tf_op | source)
XLA Modules:
  0.0 25.8 jit_solution(13739048881813846085)
XLA Ops:
  0.6 21.0 %shard_map.112 = (f32[3,4,64,128]{3,2,1,0:T(8,128)S(1)}, f32[3,4,64,128]{3,2,1,0:T(8,128)S(1)}, f32[64,128]{1,0:T(8,128)S(1)}) custom-call(f32[3,4,64,128]{3,2,1,0:T(8,128)} %adj_e.1, f32[3,4,64,128]{3,2,1,0:T(8,128)} %adj_h.1, bf16[2,3,4,64,128]{4,3,2,1,0:T(8,128)(2,1)} %saved.1, s32[4,64,128]{2,1,0:T(8,128)} %labels.1, f32[4]{0:T(128)} %eps_table.1, ...), custom_call_target="tpu_custom_call" | custom-call | tf_op jit(solution)/shard_map/pallas_call | solution.py:527
  21.7 0.0 copy-start
  21.7 0.7 %copy-done = f32[3,4,64,128]{3,2,1,0:T(8,128)} copy-done((f32[3,4,64,128]{3,2,1,0:T(8,128)}, f32[3,4,64,128]{3,2,1,0:T(8,128)S(1)}, u32[]{:S(2)}) %copy-start) | copy-done | bytes 393240
  22.4 0.0 copy-start.1
  22.4 0.7 %copy-done.1 = f32[3,4,64,128]{3,2,1,0:T(8,128)} copy-done((f32[3,4,64,128]{3,2,1,0:T(8,128)}, f32[3,4,64,128]{3,2,1,0:T(8,128)S(1)}, u32[]{:S(2)}) %copy-start.1) | copy-done | bytes 393240
  23.2 0.0 copy-start.2
  23.2 0.6 %copy-done.2 = f32[64,128]{1,0:T(8,128)} copy-done((f32[64,128]{1,0:T(8,128)}, f32[64,128]{1,0:T(8,128)S(1)}, u32[]{:S(2)}) %copy-start.2) | copy-done | bytes 32792
  23.8 2.0 %shard_map.113 = (f32[3,4,64,128]{3,2,1,0:T(8,128)}, f32[3,4,64,128]{3,2,1,0:T(8,128)}, f32[64,128]{1,0:T(8,128)}) custom-call(f32[3,4,64,128]{3,2,1,0:T(8,128)} %copy-done, f32[3,4,64,128]{3,2,1,0:T(8,128)} %copy-done.1, f32[64,128]{1,0:T(8,128)} %copy-done.2), custom_call_target="tpu_custom_call" | custom-call | tf_op jit(solution)/shard_map/pallas_call | solution.py:551
Async XLA Ops:
  21.7 0.8 %copy-start = (f32[3,4,64,128]{3,2,1,0:T(8,128)}, f32[3,4,64,128]{3,2,1,0:T(8,128)S(1)}, u32[]{:S(2)}) copy-start(f32[3,4,64,128]{3,2,1,0:T(8,128)S(1)} %get-tuple-element.6.e) | copy-start | bytes 1179652
  22.4 0.7 %copy-start.1 = (f32[3,4,64,128]{3,2,1,0:T(8,128)}, f32[3,4,64,128]{3,2,1,0:T(8,128)S(1)}, u32[]{:S(2)}) copy-start(f32[3,4,64,128]{3,2,1,0:T(8,128)S(1)} %get-tuple-element.7.h) | copy-start | bytes 1179652
  23.2 0.6 %copy-start.2 = (f32[64,128]{1,0:T(8,128)}, f32[64,128]{1,0:T(8,128)S(1)}, u32[]{:S(2)}) copy-start(f32[64,128]{1,0:T(8,128)S(1)} %get-tuple-element.8.g) | copy-start | bytes 98308

commit v3 on v2

--- a/solution.py
+++ b/solution.py
@@ -68,9 +68,7 @@
     dens_lo,
     dens_hi,
     deriv,
-    hz,
-    hr_out,
-    hr,
+    hz_out,
     zl,
     zu,
     rl_out,
@@ -93,7 +91,7 @@
     steps, comps, depth, rows, width = sv.shape
     regions = eps_table.shape[0]
     entries = cl.shape[1]
-    last = steps - 1
+    last, top = steps - 1, depth - 1
     devices = n_lat * n_ha
     lat = lax.axis_index("lat")
     ha = lax.axis_index("ha")
@@ -196,13 +194,6 @@
     pl.semaphore_wait(barrier, devices - 1)
     power_in = [exchange(pw_out, pw_in.at[d - 1], peer(d)) for d in range(1, devices)]
 
-    loads[4].wait()
-    for c in range(1, comps):
-        for z in range(depth):
-            slot = (c - 1) * depth + z
-            hr_out[slot : slot + 1, :] = h0[c, z, 0:1]
-    hz_in = exchange(h0.at[pl.ds(0, 2), 0], hz.at[steps], (lat, ha_prev), ha_dn, ha_up)
-    hr_in = exchange(hr_out, hr.at[steps], (lat_prev, ha), lat_dn, lat_up)
     loads[6].wait()
     dens_lo_in = exchange(
         dens.at[pl.ds(rows - 2 * RADIUS, 2 * RADIUS)], dens_lo, (lat_next, ha), lat_up, lat_dn
@@ -225,6 +216,7 @@
                 f = field(k, c, z)
                 rinv[k, c, z] = 1.0 / (eps + chi * f * f)
 
+    loads[4].wait()
     loads[5].wait()
     for arrive in power_in:
         arrive()
@@ -236,15 +228,11 @@
 
     lane = lax.broadcasted_iota(jnp.int32, (rows, width), 1)
     row = lax.broadcasted_iota(jnp.int32, (rows, width), 0)
-    lane_few = lax.broadcasted_iota(jnp.int32, (depth, width), 1)
     inside_ha = ha_up.astype(jnp.float32)
     inside_lat = lat_up.astype(jnp.float32)
 
     def y_lower(v):
         return jnp.where(lane == 0, 0.0, pltpu.roll(v, 1, 1))
-
-    def y_lower_few(v):
-        return jnp.where(lane_few == 0, 0.0, pltpu.roll(v, 1, 1))
 
     def y_upper(v):
         return jnp.where(lane == width - 1, 0.0, pltpu.roll(v, width - 1, 1))
@@ -265,27 +253,50 @@
             e[c, z] = now
             s[k, c, z] = value
             inner = inner + value * f
-            slot = c * depth + z
-            ru_out[k, slot : slot + 1, :] = value[0:1]
             if c > 0:
-                slot = slot - depth
+                slot = (c - 1) * depth + z
                 rl_out[k, slot : slot + 1, :] = value[rows - 1 : rows]
-            if c == 0 and z == depth - 1:
+            if c == 0 and z == top:
                 ca_out[k] = value[0:1]
             if c == 2 and z == 0:
                 cb_out[k] = value[rows - 1 : rows]
         return acc + jnp.where(lb[z] == 0, inner, 0.0)
 
+    def magnetic(k):
+        return out_h if k == 0 else hh.at[k]
+
+    def lower_layer(k, z):
+        old = h0 if k == last else magnetic(k + 1)
+        new = magnetic(k)
+        sx, sy, sz = s[k, 0, z], s[k, 1, z], s[k, 2, z]
+        curl_x = sz - y_lower(sz) - sy
+        curl_y = sx - (sz - x_lower(sz, 0.0))
+        curl_z = sy - x_lower(sy, 0.0) - (sx - y_lower(sx))
+        if z > 0:
+            curl_x = curl_x + s[k, 1, z - 1]
+            curl_y = curl_y - s[k, 0, z - 1]
+        values = (
+            old[0, z] - time_step * curl_x,
+            old[1, z] - time_step * curl_y,
+            old[2, z] - time_step * curl_z,
+        )
+        for c in range(comps):
+            new[c, z] = values[c]
+            if z == 0 and c < 2:
+                hz_out[k, c] = values[c]
+            if c > 0:
+                slot = (c - 1) * depth + z
+                ru_out[k, slot : slot + 1, :] = values[c][0:1]
+
     def send_bottom(k):
-        return exchange(s.at[k, :, 0], zu.at[k], (lat, ha_prev), ha_dn, ha_up)
+        return exchange(hz_out.at[k], zu.at[k], (lat, ha_prev), ha_dn, ha_up)
 
     def send_top(k):
-        return exchange(s.at[k, pl.ds(0, 2), depth - 1], zl.at[k], (lat, ha_next), ha_up, ha_dn)
-
-    def send_rows(k):
+        return exchange(s.at[k, pl.ds(0, 2), top], zl.at[k], (lat, ha_next), ha_up, ha_dn)
+
+    def send_edges(k):
         return (
             exchange(rl_out.at[k], rl.at[k], (lat_next, ha), lat_up, lat_dn),
-            exchange(ru_out.at[k], ru.at[k], (lat_prev, ha), lat_dn, lat_up),
             exchange(
                 ca_out.at[k],
                 ca.at[k],
@@ -302,150 +313,118 @@
             ),
         )
 
+    def send_plane(acc):
+        plane[...] = acc
+        arrivals = []
+        for d in range(n_ha):
+            other = lax.rem(ha + d, n_ha)
+            if d > 0:
+                arrivals.append(exchange(plane, plane_ha.at[d - 1], (lat, other)))
+            arrivals.append(
+                exchange(
+                    plane.at[pl.ds(rows - RADIUS, RADIUS)],
+                    plane_lo.at[d],
+                    (lat_next, other),
+                    lat_up,
+                    lat_dn,
+                )
+            )
+            arrivals.append(
+                exchange(
+                    plane.at[pl.ds(0, RADIUS)],
+                    plane_hi.at[d],
+                    (lat_prev, other),
+                    lat_dn,
+                    lat_up,
+                )
+            )
+        return arrivals
+
     acc = jnp.zeros((rows, width), jnp.float32)
-    order = [0] + ([depth - 1] if depth > 1 else []) + list(range(1, depth - 1))
-    for z in order:
+    for z in [0] + list(range(top, 0, -1)):
         acc = scale_layer(last, z, [e[c, z] for c in range(comps)], acc)
         if z == 0:
+            lower_layer(last, 0)
             zu_in = send_bottom(last)
-        if z == depth - 1:
+        if z == top:
             zl_in = send_top(last)
-    rl_in, ru_in, ca_in, cb_in = send_rows(last)
-
-    dens_lo_in()
-    dens_hi_in()
-    extended = jnp.concatenate([dens_lo[...], dens[...], dens_hi[...]], 0)
-    filtered = filter_rows(extended, rows + 2 * RADIUS)
-    slope = jnp.tanh(sharpness * (filtered - threshold))
-    deriv[...] = (
-        sharpness
-        * (1.0 - slope * slope)
-        / (jnp.tanh(sharpness * threshold) + jnp.tanh(sharpness * (1.0 - threshold)))
-    )
-    hz_in()
-    hr_in()
 
     for k in reversed(range(steps)):
-
-        def before(c, z):
-            return h0[c, z] if k == last else hh[k + 1, c, z]
-
-        def put(c, z, value):
-            if k == 0:
-                out_h[c, z] = value
-            else:
-                hh[k, c, z] = value
-
-        def after(c, z):
-            return out_h[c, z] if k == 0 else hh[k, c, z]
-
-        def lower_layer(z, below_x, below_y):
-            sx, sy, sz = s[k, 0, z], s[k, 1, z], s[k, 2, z]
-            edge_y = low_rows[z : z + 1]
-            edge_z = low_rows[depth + z : depth + z + 1]
-            curl_x = sz - y_lower(sz) - (sy - below_y)
-            curl_y = sx - below_x - (sz - x_lower(sz, edge_z))
-            curl_z = sy - x_lower(sy, edge_y) - (sx - y_lower(sx))
-            put(0, z, before(0, z) - time_step * curl_x)
-            put(1, z, before(1, z) - time_step * curl_y)
-            put(2, z, before(2, z) - time_step * curl_z)
-
+        rl_in, ca_in, cb_in = send_edges(k)
+        if k == 0:
+            plane_in = send_plane(acc)
+        for z in range(1, depth):
+            lower_layer(k, z)
+        ru_in = exchange(ru_out.at[k], ru.at[k], (lat_prev, ha), lat_dn, lat_up)
+
+        if k == last:
+            dens_lo_in()
+            dens_hi_in()
+            extended = jnp.concatenate([dens_lo[...], dens[...], dens_hi[...]], 0)
+            filtered = filter_rows(extended, rows + 2 * RADIUS)
+            slope = jnp.tanh(sharpness * (filtered - threshold))
+            deriv[...] = (
+                sharpness
+                * (1.0 - slope * slope)
+                / (jnp.tanh(sharpness * threshold) + jnp.tanh(sharpness * (1.0 - threshold)))
+            )
+
+        new = magnetic(k)
         rl_in()
-        low_rows = rl[k]
-        for z in range(1, depth):
-            lower_layer(z, s[k, 0, z - 1], s[k, 1, z - 1])
+        for z in range(depth):
+            new[1, z, 0:1] = new[1, z, 0:1] - time_step * rl[k, depth + z : depth + z + 1, :]
+            new[2, z, 0:1] = new[2, z, 0:1] + time_step * rl[k, z : z + 1, :]
 
         ru_in()
         ca_in()
-        hx_rows = ru[k, pl.ds(0, depth), :]
-        hy_rows = ru[k, pl.ds(depth, depth), :]
-        hz_rows = ru[k, pl.ds(2 * depth, depth), :]
         own_y = jnp.concatenate([s[k, 1, z, rows - 1 : rows] for z in range(depth)], 0)
         own_z = jnp.concatenate([s[k, 2, z, rows - 1 : rows] for z in range(depth)], 0)
-        under = ca[k]
-        if depth > 1:
-            under = jnp.concatenate([under, hx_rows[0 : depth - 1]], 0)
-        old_y = hr[k + 1, pl.ds(0, depth), :]
-        old_z = hr[k + 1, pl.ds(depth, depth), :]
-        high_y = old_y - time_step * (hx_rows - under - (hz_rows - own_z))
-        high_z = old_z - time_step * (hy_rows - own_y - (hx_rows - y_lower_few(hx_rows)))
-        high_y = high_y * inside_lat
-        high_z = high_z * inside_lat
-        hr[k, pl.ds(0, depth), :] = high_y
-        hr[k, pl.ds(depth, depth), :] = high_z
-
-        zl_in()
-        lower_layer(0, zl[k, 0], zl[k, 1])
-
-        def upper_layer(z, above_x, above_y):
-            hx, hy, hv = after(0, z), after(1, z), after(2, z)
-            edge_y = high_y[z : z + 1]
+        high_y = (ru[k, pl.ds(0, depth), :] - time_step * own_z) * inside_lat
+        high_z = (ru[k, pl.ds(depth, depth), :] + time_step * own_y) * inside_lat
+        first_y = high_y[0:1] + time_step * inside_lat * ca[k]
+
+        def finish_layer(z, above_x, above_y, acc):
+            hx, hy, hv = new[0, z], new[1, z], new[2, z]
+            edge_y = first_y if z == 0 else high_y[z : z + 1]
             edge_z = high_z[z : z + 1]
             curl_x = y_upper(hv) - hv - (above_y - hy)
             curl_y = above_x - hx - (x_upper(hv, edge_z) - hv)
             curl_z = x_upper(hy, edge_y) - hy - (y_upper(hx) - hx)
-            return (
+            fields = (
                 e[0, z] + time_step * curl_x,
                 e[1, z] + time_step * curl_y,
                 e[2, z] + time_step * curl_z,
             )
-
-        def finish_layer(z, above_x, above_y, acc):
-            fields = upper_layer(z, above_x, above_y)
             if k > 0:
                 return scale_layer(k - 1, z, fields, acc)
             for c in range(comps):
                 out_e[c, z] = fields[c]
             return acc
 
-        for z in range(depth - 1):
-            acc = finish_layer(z, after(0, z + 1), after(1, z + 1), acc)
-            if z == 0 and k > 0:
+        for z in range(1, top):
+            acc = finish_layer(z, new[0, z + 1], new[1, z + 1], acc)
+
+        zl_in()
+        new[0, 0] = new[0, 0] - time_step * zl[k, 1]
+        new[1, 0] = new[1, 0] + time_step * zl[k, 0]
+        if top > 0:
+            acc = finish_layer(0, new[0, 1], new[1, 1], acc)
+            if k > 0:
+                lower_layer(k - 1, 0)
                 zu_next = send_bottom(k - 1)
 
         zu_in()
         cb_in()
-        top = depth - 1
-        nx, ny, nz = zu[k, 0], zu[k, 1], zu[k, 2]
-        above_x = hz[k + 1, 0] - time_step * (nz - y_lower(nz) - (ny - s[k, 1, top]))
-        above_y = hz[k + 1, 1] - time_step * (nx - s[k, 0, top] - (nz - x_lower(nz, cb[k])))
-        above_x = above_x * inside_ha
-        above_y = above_y * inside_ha
-        hz[k, 0] = above_x
-        hz[k, 1] = above_y
-        acc = finish_layer(top, above_x, above_y, acc)
-
+        above_x = zu[k, 0] - time_step * s[k, 1, top]
+        above_y = zu[k, 1] + time_step * s[k, 0, top]
+        above_y = above_y - jnp.where(row == 0, time_step * cb[k], 0.0)
+        acc = finish_layer(top, above_x * inside_ha, above_y * inside_ha, acc)
         if k > 0:
-            if depth == 1:
+            if top == 0:
+                lower_layer(k - 1, 0)
                 zu_next = send_bottom(k - 1)
             zu_in = zu_next
             zl_in = send_top(k - 1)
-            rl_in, ru_in, ca_in, cb_in = send_rows(k - 1)
-        if k == min(1, last):
-            plane[...] = acc
-            plane_in = []
-            for d in range(n_ha):
-                other = lax.rem(ha + d, n_ha)
-                if d > 0:
-                    plane_in.append(exchange(plane, plane_ha.at[d - 1], (lat, other)))
-                plane_in.append(
-                    exchange(
-                        plane.at[pl.ds(rows - RADIUS, RADIUS)],
-                        plane_lo.at[d],
-                        (lat_next, other),
-                        lat_up,
-                        lat_dn,
-                    )
-                )
-                plane_in.append(
-                    exchange(
-                        plane.at[pl.ds(0, RADIUS)],
-                        plane_hi.at[d],
-                        (lat_prev, other),
-                        lat_dn,
-                        lat_up,
-                    )
-                )
 
     for arrive in plane_in:
         arrive()
@@ -482,7 +461,7 @@
     entries = mon_cells.shape[0]
     f32 = jnp.float32
     block = (comps, depth, rows, width)
-    copies = (n_lat * n_ha - 1) + 4 + 6 * steps + 3 * n_ha - 1
+    copies = (n_lat * n_ha - 1) + 2 + 6 * steps + 3 * n_ha - 1
     vmem = pl.BlockSpec(memory_space=pltpu.VMEM)
     hbm = pl.BlockSpec(memory_space=pltpu.HBM)
     scalars = pl.BlockSpec(memory_space=pltpu.SMEM)
@@ -502,15 +481,13 @@
         pltpu.VMEM((2 * RADIUS, width), f32),
         pltpu.VMEM((2 * RADIUS, width), f32),
         pltpu.VMEM((rows + 2 * RADIUS, width), f32),
-        pltpu.VMEM((steps + 1, 2, rows, width), f32),
-        pltpu.VMEM((2 * depth, width), f32),
-        pltpu.VMEM((steps + 1, 2 * depth, width), f32),
         pltpu.VMEM((steps, 2, rows, width), f32),
-        pltpu.VMEM((steps, 3, rows, width), f32),
+        pltpu.VMEM((steps, 2, rows, width), f32),
+        pltpu.VMEM((steps, 2, rows, width), f32),
         pltpu.VMEM((steps, 2 * depth, width), f32),
         pltpu.VMEM((steps, 2 * depth, width), f32),
-        pltpu.VMEM((steps, 3 * depth, width), f32),
-        pltpu.VMEM((steps, 3 * depth, width), f32),
+        pltpu.VMEM((steps, 2 * depth, width), f32),
+        pltpu.VMEM((steps, 2 * depth, width), f32),
         pltpu.VMEM((steps, 1, width), f32),
         pltpu.VMEM((steps, 1, width), f32),
         pltpu.VMEM((steps, 1, width), f32),
@@ -558,6 +535,7 @@
         in_specs=[vmem] * 3,
         out_specs=(hbm, hbm, hbm),
         scratch_shapes=[pltpu.SemaphoreType.DMA((3,))],
+        compiler_params=pltpu.CompilerParams(vmem_limit_bytes=2**20),
     )(*results)
 
 

time: 26 us -> 22.1 us (0.85)
  local copies, waits for them, and re-layouts: 2.09 us -> 0 us
  Pallas kernels: 23 us -> 21.3 us
    unnamed x6 -> x0, local copies, waits for them, and re-layouts: 2.09 us -> none
    pallas_call x1, Pallas kernels: 2.02 us -> 0.91 us  [body(): pl.pallas_call(store, out_shape=(jax.ShapeDtypeStruct(block, f32), jax.Sh...]
    pallas_call x1, Pallas kernels: 21 us -> 20.4 us  [body(): pl.pallas_call(functools.partial(kernel, n_lat, n_ha), out_shape=(pltpu.V...]
where the time goes in v3:
time: 22.1 us; the launch traced here: 21.9 us
  Pallas kernels  21.3 us (96%)
  between operations  0.64 us (3%)
    pallas_call x1, Pallas kernels, body(): pl.pallas_call(functools.partial(kernel, n_lat, n_ha), out_shape=(pltpu.V...  20.4 us
    pallas_call x1, Pallas kernels, body(): pl.pallas_call(store, out_shape=(jax.ShapeDtypeStruct(block, f32), jax.Sh...  0.91 us

profile of v3, /device:TPU:0, one launch (start us, length us, event | category | flops | bytes accessed | tf_op | source)
XLA Modules:
  0.0 21.9 jit_solution(17197393704969178848)
XLA Ops:
  0.6 20.4 %shard_map.112 = (f32[3,4,64,128]{3,2,1,0:T(8,128)S(1)}, f32[3,4,64,128]{3,2,1,0:T(8,128)S(1)}, f32[64,128]{1,0:T(8,128)S(1)}) custom-call(f32[3,4,64,128]{3,2,1,0:T(8,128)} %adj_e.1, f32[3,4,64,128]{3,2,1,0:T(8,128)} %adj_h.1, bf16[2,3,4,64,128]{4,3,2,1,0:T(8,128)(2,1)} %saved.1, s32[4,64,128]{2,1,0:T(8,128)} %labels.1, f32[4]{0:T(128)} %eps_table.1, ...), custom_call_target="tpu_custom_call" | custom-call | tf_op jit(solution)/shard_map/pallas_call | solution.py:504
  21.0 0.9 %shard_map.113 = (f32[3,4,64,128]{3,2,1,0:T(8,128)}, f32[3,4,64,128]{3,2,1,0:T(8,128)}, f32[64,128]{1,0:T(8,128)}) custom-call(f32[3,4,64,128]{3,2,1,0:T(8,128)S(1)} %get-tuple-element.6.e, f32[3,4,64,128]{3,2,1,0:T(8,128)S(1)} %get-tuple-element.7.h, f32[64,128]{1,0:T(8,128)S(1)} %get-tuple-element.8.g), custom_call_target="tpu_custom_call" | custom-call | tf_op jit(solution)/shard_map/pallas_call | solution.py:528

commit v4 on v3

--- a/solution.py
+++ b/solution.py
@@ -81,6 +81,21 @@
     cb,
     pw_out,
     pw_in,
+    pw_sum,
+    pw_all,
+    ab,
+    pab,
+    hzab_out,
+    zuab,
+    zlab,
+    rlab_out,
+    rlab,
+    ruab_out,
+    ruab,
+    caab_out,
+    caab,
+    cbab_out,
+    cbab,
     plane_ha,
     plane_lo,
     plane_hi,
@@ -113,19 +128,47 @@
     for load in loads:
         load.start()
 
+    group = 2 if n_lat % 2 == 0 else 1
+    place, number = lax.rem(lat, group), lax.div(lat, group)
+    members, groups = group * n_ha, n_lat // group
+
+    def member(d):
+        there = lax.rem(place * n_ha + ha + d, members)
+        return (number * group + lax.div(there, n_ha), lax.rem(there, n_ha))
+
+    def counterpart(d):
+        return (lax.rem(number + d, groups) * group + place, ha)
+
     barrier = pltpu.get_barrier_semaphore()
 
-    def peer(d):
-        there = lax.rem(lat * n_ha + ha + d, devices)
-        return (lax.div(there, n_ha), lax.rem(there, n_ha))
-
-    for d in range(1, devices):
-        pl.semaphore_signal(barrier, inc=1, device_id=peer(d), device_id_type=MESH)
+    def greet(target):
+        pl.semaphore_signal(barrier, inc=1, device_id=target, device_id_type=MESH)
+
+    for d in range(1, members):
+        greet(member(d))
+    for d in range(1, groups):
+        greet(counterpart(d))
+    greeted = (members - 1) + (groups - 1)
+    if group == 2:
+        outer = lat - 1 + 2 * place
+        exists = jnp.logical_and(outer >= 0, outer < n_lat)
+        beyond = [(exists, outer, d) for d in range(n_ha)]
+    else:
+        beyond = [(lat_dn, lat_prev, d) for d in range(1, n_ha)]
+        beyond += [(lat_up, lat_next, d) for d in range(1, n_ha)]
+    for condition, there, d in beyond:
+        pl.when(condition)(functools.partial(greet, (there, lax.rem(ha + d, n_ha))))
+        greeted = greeted + condition.astype(jnp.int32)
 
     issued = []
+    numbers = iter(range(send_sem.shape[0]))
+
+    def finish_sends(kept=0):
+        while len(issued) > kept:
+            issued.pop(0)()
 
     def exchange(src, dst, target, sends=None, receives=None):
-        index = len(issued)
+        index = next(numbers)
 
         def copy():
             return pltpu.make_async_remote_copy(
@@ -191,8 +234,114 @@
             acc = acc + wgrid[z] * square
         pw_out[k : k + 1, :] = jnp.sum(acc, 0, keepdims=True)
 
-    pl.semaphore_wait(barrier, devices - 1)
-    power_in = [exchange(pw_out, pw_in.at[d - 1], peer(d)) for d in range(1, devices)]
+    pl.semaphore_wait(barrier, greeted)
+    members_in = [exchange(pw_out, pw_in.at[d - 1], member(d)) for d in range(1, members)]
+
+    lane = lax.broadcasted_iota(jnp.int32, (rows, width), 1)
+    row = lax.broadcasted_iota(jnp.int32, (rows, width), 0)
+    inside_ha = ha_up.astype(jnp.float32)
+    inside_lat = lat_up.astype(jnp.float32)
+
+    def y_lower(v):
+        return jnp.where(lane == 0, 0.0, pltpu.roll(v, 1, 1))
+
+    def y_upper(v):
+        return jnp.where(lane == width - 1, 0.0, pltpu.roll(v, width - 1, 1))
+
+    def x_lower(v, edge):
+        return jnp.where(row == 0, edge, pltpu.roll(v, 1, 0))
+
+    def x_upper(v, edge):
+        return jnp.where(row == rows - 1, edge, pltpu.roll(v, rows - 1, 0))
+
+    def material(z):
+        label = lb[z]
+        eps = jnp.full((rows, width), eps_table[0], jnp.float32)
+        chi = jnp.full((rows, width), 3.0 * chi_table[0], jnp.float32)
+        for region in range(1, regions):
+            hit = label == region
+            eps = jnp.where(hit, eps_table[region], eps)
+            chi = jnp.where(hit, 3.0 * chi_table[region], chi)
+        return eps, chi
+
+    def lower_parts(src, z):
+        sx, sy, sz = src[0, z], src[1, z], src[2, z]
+        curl_x = sz - y_lower(sz) - sy
+        curl_y = sx - (sz - x_lower(sz, 0.0))
+        curl_z = sy - x_lower(sy, 0.0) - (sx - y_lower(sx))
+        if z > 0:
+            curl_x = curl_x + src[1, z - 1]
+            curl_y = curl_y - src[0, z - 1]
+        return curl_x, curl_y, curl_z
+
+    def both_parts(z):
+        eps, chi = material(z)
+        inner = [jnp.zeros((rows, width), jnp.float32) for _ in range(2)]
+        for c in range(comps):
+            f = field(last, c, z)
+            inverse = 1.0 / (eps + chi * f * f)
+            for i, value in enumerate((e[c, z] * inverse, wgrid[z] * f * inverse)):
+                ab[i, c, z] = value
+                inner[i] = inner[i] + value * f
+                if c > 0:
+                    slot = (2 * i + c - 1) * depth + z
+                    rlab_out[slot : slot + 1, :] = value[rows - 1 : rows]
+                if c == 0 and z == top:
+                    caab_out[i : i + 1, :] = value[0:1]
+                if c == 2 and z == 0:
+                    cbab_out[i : i + 1, :] = value[rows - 1 : rows]
+        return [jnp.where(lb[z] == 0, value, 0.0) for value in inner]
+
+    def both_curls(z):
+        for i in range(2):
+            curl = lower_parts(ab.at[i], z)
+            for c in range(comps):
+                value = -time_step * curl[c]
+                if i == 0:
+                    value = h0[c, z] + value
+                pab[i, c, z] = value
+                if z == 0 and c < 2:
+                    hzab_out[i, c] = value
+                if c > 0:
+                    slot = (2 * i + c - 1) * depth + z
+                    ruab_out[slot : slot + 1, :] = value[0:1]
+
+    loads[3].wait()
+    loads[4].wait()
+    loads[5].wait()
+    inner = [jnp.zeros((rows, width), jnp.float32) for _ in range(2)]
+    for z in [0] + list(range(top, 0, -1)):
+        inner = [old + more for old, more in zip(inner, both_parts(z))]
+        if z == 0:
+            both_curls(0)
+            zuab_in = exchange(hzab_out, zuab, (lat, ha_prev), ha_dn, ha_up)
+        if z == top:
+            zlab_in = exchange(ab.at[:, pl.ds(0, 2), top], zlab, (lat, ha_next), ha_up, ha_dn)
+    corner_a = (
+        (lat_prev, ha_next),
+        jnp.logical_and(lat_dn, ha_up),
+        jnp.logical_and(lat_up, ha_dn),
+    )
+    corner_b = (
+        (lat_next, ha_prev),
+        jnp.logical_and(lat_up, ha_dn),
+        jnp.logical_and(lat_dn, ha_up),
+    )
+    rlab_in = exchange(rlab_out, rlab, (lat_next, ha), lat_up, lat_dn)
+    caab_in = exchange(caab_out, caab, *corner_a)
+    cbab_in = exchange(cbab_out, cbab, *corner_b)
+
+    for arrive in members_in:
+        arrive()
+    power_rows = pw_out[...]
+    for d in range(1, members):
+        power_rows = power_rows + pw_in[d - 1]
+    pw_sum[...] = power_rows
+    groups_in = [exchange(pw_sum, pw_all.at[d - 1], counterpart(d)) for d in range(1, groups)]
+
+    for z in range(1, depth):
+        both_curls(z)
+    ruab_in = exchange(ruab_out, ruab, (lat_prev, ha), lat_dn, lat_up)
 
     loads[6].wait()
     dens_lo_in = exchange(
@@ -202,46 +351,19 @@
         dens.at[pl.ds(0, 2 * RADIUS)], dens_hi, (lat_prev, ha), lat_dn, lat_up
     )
 
-    loads[3].wait()
     for z in range(depth):
-        label = lb[z]
-        eps = jnp.full((rows, width), eps_table[0], jnp.float32)
-        chi = jnp.full((rows, width), 3.0 * chi_table[0], jnp.float32)
-        for region in range(1, regions):
-            member = label == region
-            eps = jnp.where(member, eps_table[region], eps)
-            chi = jnp.where(member, 3.0 * chi_table[region], chi)
-        for k in range(steps):
+        eps, chi = material(z)
+        for k in range(last):
             for c in range(comps):
                 f = field(k, c, z)
                 rinv[k, c, z] = 1.0 / (eps + chi * f * f)
 
-    loads[4].wait()
-    loads[5].wait()
-    for arrive in power_in:
+    for arrive in groups_in:
         arrive()
-    power_rows = pw_out[...]
-    for d in range(1, devices):
-        power_rows = power_rows + pw_in[d - 1]
+    for d in range(1, groups):
+        power_rows = power_rows + pw_all[d - 1]
     power = jnp.sum(power_rows, 1, keepdims=True) / (entries * devices) + epsilon
     inverse_power = 1.0 / power
-
-    lane = lax.broadcasted_iota(jnp.int32, (rows, width), 1)
-    row = lax.broadcasted_iota(jnp.int32, (rows, width), 0)
-    inside_ha = ha_up.astype(jnp.float32)
-    inside_lat = lat_up.astype(jnp.float32)
-
-    def y_lower(v):
-        return jnp.where(lane == 0, 0.0, pltpu.roll(v, 1, 1))
-
-    def y_upper(v):
-        return jnp.where(lane == width - 1, 0.0, pltpu.roll(v, width - 1, 1))
-
-    def x_lower(v, edge):
-        return jnp.where(row == 0, edge, pltpu.roll(v, 1, 0))
-
-    def x_upper(v, edge):
-        return jnp.where(row == rows - 1, edge, pltpu.roll(v, rows - 1, 0))
 
     def scale_layer(k, z, fields, acc):
         gain = inverse_power[k : k + 1, :]
@@ -266,15 +388,9 @@
         return out_h if k == 0 else hh.at[k]
 
     def lower_layer(k, z):
-        old = h0 if k == last else magnetic(k + 1)
+        old = magnetic(k + 1)
         new = magnetic(k)
-        sx, sy, sz = s[k, 0, z], s[k, 1, z], s[k, 2, z]
-        curl_x = sz - y_lower(sz) - sy
-        curl_y = sx - (sz - x_lower(sz, 0.0))
-        curl_z = sy - x_lower(sy, 0.0) - (sx - y_lower(sx))
-        if z > 0:
-            curl_x = curl_x + s[k, 1, z - 1]
-            curl_y = curl_y - s[k, 0, z - 1]
+        curl_x, curl_y, curl_z = lower_parts(s.at[k], z)
         values = (
             old[0, z] - time_step * curl_x,
             old[1, z] - time_step * curl_y,
@@ -297,20 +413,8 @@
     def send_edges(k):
         return (
             exchange(rl_out.at[k], rl.at[k], (lat_next, ha), lat_up, lat_dn),
-            exchange(
-                ca_out.at[k],
-                ca.at[k],
-                (lat_prev, ha_next),
-                jnp.logical_and(lat_dn, ha_up),
-                jnp.logical_and(lat_up, ha_dn),
-            ),
-            exchange(
-                cb_out.at[k],
-                cb.at[k],
-                (lat_next, ha_prev),
-                jnp.logical_and(lat_up, ha_dn),
-                jnp.logical_and(lat_dn, ha_up),
-            ),
+            exchange(ca_out.at[k], ca.at[k], *corner_a),
+            exchange(cb_out.at[k], cb.at[k], *corner_b),
         )
 
     def send_plane(acc):
@@ -340,22 +444,35 @@
             )
         return arrivals
 
-    acc = jnp.zeros((rows, width), jnp.float32)
-    for z in [0] + list(range(top, 0, -1)):
-        acc = scale_layer(last, z, [e[c, z] for c in range(comps)], acc)
-        if z == 0:
-            lower_layer(last, 0)
-            zu_in = send_bottom(last)
-        if z == top:
-            zl_in = send_top(last)
+    gain = inverse_power[last : last + 1, :]
+    acc = inner[0] + gain * inner[1]
+    for z in range(depth):
+        for c in range(comps):
+            magnetic(last)[c, z] = pab[0, c, z] + gain * pab[1, c, z]
+
+    def joined(ref):
+        half = ref.shape[0] // 2
+        return ref[pl.ds(0, half)] + gain * ref[pl.ds(half, half)]
 
     for k in reversed(range(steps)):
-        rl_in, ca_in, cb_in = send_edges(k)
-        if k == 0:
-            plane_in = send_plane(acc)
-        for z in range(1, depth):
-            lower_layer(k, z)
-        ru_in = exchange(ru_out.at[k], ru.at[k], (lat_prev, ha), lat_dn, lat_up)
+        if k == last:
+            rl_in, ru_in, zl_in, zu_in, ca_in, cb_in = (
+                rlab_in,
+                ruab_in,
+                zlab_in,
+                zuab_in,
+                caab_in,
+                cbab_in,
+            )
+        else:
+            kept = len(issued)
+            rl_in, ca_in, cb_in = send_edges(k)
+            if k == 0:
+                plane_in = send_plane(acc)
+            for z in range(1, depth):
+                lower_layer(k, z)
+            ru_in = exchange(ru_out.at[k], ru.at[k], (lat_prev, ha), lat_dn, lat_up)
+            finish_sends(len(issued) - kept + 2)
 
         if k == last:
             dens_lo_in()
@@ -371,17 +488,19 @@
 
         new = magnetic(k)
         rl_in()
+        low = joined(rlab) if k == last else rl[k]
         for z in range(depth):
-            new[1, z, 0:1] = new[1, z, 0:1] - time_step * rl[k, depth + z : depth + z + 1, :]
-            new[2, z, 0:1] = new[2, z, 0:1] + time_step * rl[k, z : z + 1, :]
+            new[1, z, 0:1] = new[1, z, 0:1] - time_step * low[depth + z : depth + z + 1]
+            new[2, z, 0:1] = new[2, z, 0:1] + time_step * low[z : z + 1]
 
         ru_in()
         ca_in()
-        own_y = jnp.concatenate([s[k, 1, z, rows - 1 : rows] for z in range(depth)], 0)
-        own_z = jnp.concatenate([s[k, 2, z, rows - 1 : rows] for z in range(depth)], 0)
-        high_y = (ru[k, pl.ds(0, depth), :] - time_step * own_z) * inside_lat
-        high_z = (ru[k, pl.ds(depth, depth), :] + time_step * own_y) * inside_lat
-        first_y = high_y[0:1] + time_step * inside_lat * ca[k]
+        own = joined(rlab_out) if k == last else rl_out[k]
+        high = joined(ruab) if k == last else ru[k]
+        corner = joined(caab) if k == last else ca[k]
+        high_y = (high[0:depth] - time_step * own[depth : 2 * depth]) * inside_lat
+        high_z = (high[depth : 2 * depth] + time_step * own[0:depth]) * inside_lat
+        first_y = high_y[0:1] + time_step * inside_lat * corner
 
         def finish_layer(z, above_x, above_y, acc):
             hx, hy, hv = new[0, z], new[1, z], new[2, z]
@@ -390,11 +509,14 @@
             curl_x = y_upper(hv) - hv - (above_y - hy)
             curl_y = above_x - hx - (x_upper(hv, edge_z) - hv)
             curl_z = x_upper(hy, edge_y) - hy - (y_upper(hx) - hx)
-            fields = (
+            fields = [
                 e[0, z] + time_step * curl_x,
                 e[1, z] + time_step * curl_y,
                 e[2, z] + time_step * curl_z,
-            )
+            ]
+            if k == last:
+                for c in range(comps):
+                    fields[c] = fields[c] + gain * (wgrid[z] * field(k, c, z))
             if k > 0:
                 return scale_layer(k - 1, z, fields, acc)
             for c in range(comps):
@@ -405,8 +527,12 @@
             acc = finish_layer(z, new[0, z + 1], new[1, z + 1], acc)
 
         zl_in()
-        new[0, 0] = new[0, 0] - time_step * zl[k, 1]
-        new[1, 0] = new[1, 0] + time_step * zl[k, 0]
+        if k == last:
+            below_x, below_y = zlab[0, 0] + gain * zlab[1, 0], zlab[0, 1] + gain * zlab[1, 1]
+        else:
+            below_x, below_y = zl[k, 0], zl[k, 1]
+        new[0, 0] = new[0, 0] - time_step * below_y
+        new[1, 0] = new[1, 0] + time_step * below_x
         if top > 0:
             acc = finish_layer(0, new[0, 1], new[1, 1], acc)
             if k > 0:
@@ -415,9 +541,17 @@
 
         zu_in()
         cb_in()
-        above_x = zu[k, 0] - time_step * s[k, 1, top]
-        above_y = zu[k, 1] + time_step * s[k, 0, top]
-        above_y = above_y - jnp.where(row == 0, time_step * cb[k], 0.0)
+        if k == last:
+            above_x, above_y = zuab[0, 0] + gain * zuab[1, 0], zuab[0, 1] + gain * zuab[1, 1]
+            own_x, own_y = ab[0, 0, top] + gain * ab[1, 0, top], ab[0, 1, top] + gain * ab[1, 1, top]
+            corner = joined(cbab)
+        else:
+            above_x, above_y = zu[k, 0], zu[k, 1]
+            own_x, own_y = s[k, 0, top], s[k, 1, top]
+            corner = cb[k]
+        above_x = above_x - time_step * own_y
+        above_y = above_y + time_step * own_x
+        above_y = above_y - jnp.where(row == 0, time_step * corner, 0.0)
         acc = finish_layer(top, above_x * inside_ha, above_y * inside_ha, acc)
         if k > 0:
             if top == 0:
@@ -437,8 +571,7 @@
         high = high + plane_hi[d]
     product = jnp.concatenate([low, middle, high], 0) * deriv[...]
     out_g[...] = filter_rows(product, rows)
-    for finish in issued:
-        finish()
+    finish_sends()
 
 
 def store(e, h, g, out_e, out_h, out_g, sem):
@@ -461,7 +594,9 @@
     entries = mon_cells.shape[0]
     f32 = jnp.float32
     block = (comps, depth, rows, width)
-    copies = (n_lat * n_ha - 1) + 2 + 6 * steps + 3 * n_ha - 1
+    group = 2 if n_lat % 2 == 0 else 1
+    members, groups = group * n_ha, n_lat // group
+    copies = (members - 1) + (groups - 1) + 2 + 6 * steps + 3 * n_ha - 1
     vmem = pl.BlockSpec(memory_space=pltpu.VMEM)
     hbm = pl.BlockSpec(memory_space=pltpu.HBM)
     scalars = pl.BlockSpec(memory_space=pltpu.SMEM)
@@ -493,7 +628,22 @@
         pltpu.VMEM((steps, 1, width), f32),
         pltpu.VMEM((steps, 1, width), f32),
         pltpu.VMEM((steps, width), f32),
-        pltpu.VMEM((n_lat * n_ha - 1, steps, width), f32),
+        pltpu.VMEM((max(members - 1, 1), steps, width), f32),
+        pltpu.VMEM((steps, width), f32),
+        pltpu.VMEM((max(groups - 1, 1), steps, width), f32),
+        pltpu.VMEM((2,) + block, f32),
+        pltpu.VMEM((2,) + block, f32),
+        pltpu.VMEM((2, 2, rows, width), f32),
+        pltpu.VMEM((2, 2, rows, width), f32),
+        pltpu.VMEM((2, 2, rows, width), f32),
+        pltpu.VMEM((4 * depth, width), f32),
+        pltpu.VMEM((4 * depth, width), f32),
+        pltpu.VMEM((4 * depth, width), f32),
+        pltpu.VMEM((4 * depth, width), f32),
+        pltpu.VMEM((2, width), f32),
+        pltpu.VMEM((2, width), f32),
+        pltpu.VMEM((2, width), f32),
+        pltpu.VMEM((2, width), f32),
         pltpu.VMEM((max(n_ha - 1, 1), rows, width), f32),
         pltpu.VMEM((n_ha, RADIUS, width), f32),
         pltpu.VMEM((n_ha, RADIUS, width), f32),

time: 22.1 us -> 20.1 us (0.910)
  the two profiles are of different devices: /device:TPU:0 before, /device:TPU:1 now
where the time goes in v4:
time: 20.1 us; the launch traced here: 19.9 us
  Pallas kernels  19.2 us (96%)
  between operations  0.64 us (3%)
    pallas_call x1, Pallas kernels, body(): pl.pallas_call(functools.partial(kernel, n_lat, n_ha), out_shape=(pltpu.V...  18.3 us
    pallas_call x1, Pallas kernels, body(): pl.pallas_call(store, out_shape=(jax.ShapeDtypeStruct(block, f32), jax.Sh...  0.91 us

profile of v4, /device:TPU:1, one launch (start us, length us, event | category | flops | bytes accessed | tf_op | source)
XLA Modules:
  0.0 19.9 jit_solution(1429232720566771508)
XLA Ops:
  0.6 18.3 %shard_map.112 = (f32[3,4,64,128]{3,2,1,0:T(8,128)S(1)}, f32[3,4,64,128]{3,2,1,0:T(8,128)S(1)}, f32[64,128]{1,0:T(8,128)S(1)}) custom-call(f32[3,4,64,128]{3,2,1,0:T(8,128)} %adj_e.1, f32[3,4,64,128]{3,2,1,0:T(8,128)} %adj_h.1, bf16[2,3,4,64,128]{4,3,2,1,0:T(8,128)(2,1)} %saved.1, s32[4,64,128]{2,1,0:T(8,128)} %labels.1, f32[4]{0:T(128)} %eps_table.1, ...), custom_call_target="tpu_custom_call" | custom-call | tf_op jit(solution)/shard_map/pallas_call | solution.py:654
  19.0 0.9 %shard_map.113 = (f32[3,4,64,128]{3,2,1,0:T(8,128)}, f32[3,4,64,128]{3,2,1,0:T(8,128)}, f32[64,128]{1,0:T(8,128)}) custom-call(f32[3,4,64,128]{3,2,1,0:T(8,128)S(1)} %get-tuple-element.6.e, f32[3,4,64,128]{3,2,1,0:T(8,128)S(1)} %get-tuple-element.7.h, f32[64,128]{1,0:T(8,128)S(1)} %get-tuple-element.8.g), custom_call_target="tpu_custom_call" | custom-call | tf_op jit(solution)/shard_map/pallas_call | solution.py:678

commit v5 on v4

--- a/solution.py
+++ b/solution.py
@@ -79,6 +79,8 @@
     ca,
     cb_out,
     cb,
+    eps_of,
+    chi_of,
     pw_out,
     pw_in,
     pw_sum,
@@ -123,6 +125,8 @@
         (adj_h, h0),
         (adj_e, e),
         (density, dens),
+        (eps_table, eps_of),
+        (chi_table, chi_of),
     ]
     loads = [pltpu.make_async_copy(a, b, local_sem.at[i]) for i, (a, b) in enumerate(pairs)]
     for load in loads:
@@ -198,6 +202,105 @@
                     dst[...] = jnp.zeros(dst.shape, dst.dtype)
 
         return arrive
+
+    def field(k, c, z):
+        return sv[k, c, z].astype(jnp.float32)
+
+    lane = lax.broadcasted_iota(jnp.int32, (rows, width), 1)
+    row = lax.broadcasted_iota(jnp.int32, (rows, width), 0)
+    inside_ha = ha_up.astype(jnp.float32)
+    inside_lat = lat_up.astype(jnp.float32)
+
+    def y_lower(v):
+        return jnp.where(lane == 0, 0.0, pltpu.roll(v, 1, 1))
+
+    def y_upper(v):
+        return jnp.where(lane == width - 1, 0.0, pltpu.roll(v, width - 1, 1))
+
+    def x_lower(v, edge):
+        return jnp.where(row == 0, edge, pltpu.roll(v, 1, 0))
+
+    def x_upper(v, edge):
+        return jnp.where(row == rows - 1, edge, pltpu.roll(v, rows - 1, 0))
+
+    def material(z):
+        label = lb[z]
+        eps = jnp.full((rows, width), eps_of[0], jnp.float32)
+        chi = jnp.full((rows, width), 3.0 * chi_of[0], jnp.float32)
+        for region in range(1, regions):
+            hit = label == region
+            eps = jnp.where(hit, eps_of[region], eps)
+            chi = jnp.where(hit, 3.0 * chi_of[region], chi)
+        return eps, chi
+
+    def lower_parts(src, z):
+        sx, sy, sz = src[0, z], src[1, z], src[2, z]
+        curl_x = sz - y_lower(sz) - sy
+        curl_y = sx - (sz - x_lower(sz, 0.0))
+        curl_z = sy - x_lower(sy, 0.0) - (sx - y_lower(sx))
+        if z > 0:
+            curl_x = curl_x + src[1, z - 1]
+            curl_y = curl_y - src[0, z - 1]
+        return curl_x, curl_y, curl_z
+
+    def part_a(z):
+        eps, chi = material(z)
+        inner = jnp.zeros((rows, width), jnp.float32)
+        for c in range(comps):
+            f = field(last, c, z)
+            inverse = 1.0 / (eps + chi * f * f)
+            ab[1, c, z] = f * inverse
+            inner = inner + put_part(0, c, z, e[c, z] * inverse) * f
+        return jnp.where(lb[z] == 0, inner, 0.0)
+
+    def part_b(z):
+        inner = jnp.zeros((rows, width), jnp.float32)
+        for c in range(comps):
+            inner = inner + put_part(1, c, z, wgrid[z] * ab[1, c, z]) * field(last, c, z)
+        return jnp.where(lb[z] == 0, inner, 0.0)
+
+    def put_part(i, c, z, value):
+        ab[i, c, z] = value
+        if c > 0:
+            slot = (2 * i + c - 1) * depth + z
+            rlab_out[slot : slot + 1, :] = value[rows - 1 : rows]
+        if c == 0 and z == top:
+            caab_out[i : i + 1, :] = value[0:1]
+        if c == 2 and z == 0:
+            cbab_out[i : i + 1, :] = value[rows - 1 : rows]
+        return value
+
+    def part_curl(i, z):
+        curl = lower_parts(ab.at[i], z)
+        for c in range(comps):
+            value = -time_step * curl[c]
+            if i == 0:
+                value = h0[c, z] + value
+            pab[i, c, z] = value
+            if z == 0 and c < 2:
+                hzab_out[i, c] = value
+            if c > 0:
+                slot = (2 * i + c - 1) * depth + z
+                ruab_out[slot : slot + 1, :] = value[0:1]
+
+    def ends(part, i, wait=None):
+        inner = part(0)
+        part_curl(i, 0)
+        if wait is not None:
+            wait()
+        arrivals = [exchange(hzab_out.at[i], zuab.at[i], (lat, ha_prev), ha_dn, ha_up)]
+        if top > 0:
+            inner = inner + part(top)
+        arrivals.append(
+            exchange(ab.at[i, pl.ds(0, 2), top], zlab.at[i], (lat, ha_next), ha_up, ha_dn)
+        )
+        return inner, arrivals
+
+    for index in (2, 3, 4, 5, 7, 8):
+        loads[index].wait()
+    inner_a, (zua_in, zla_in) = ends(
+        part_a, 0, lambda: pl.semaphore_wait(barrier, greeted)
+    )
 
     loads[0].wait()
     loads[1].wait()
@@ -219,11 +322,6 @@
     for z in range(depth):
         wgrid[z] = total[z * rows : (z + 1) * rows]
 
-    loads[2].wait()
-
-    def field(k, c, z):
-        return sv[k, c, z].astype(jnp.float32)
-
     for k in range(steps):
         acc = jnp.zeros((rows, width), jnp.float32)
         for z in range(depth):
@@ -234,89 +332,12 @@
             acc = acc + wgrid[z] * square
         pw_out[k : k + 1, :] = jnp.sum(acc, 0, keepdims=True)
 
-    pl.semaphore_wait(barrier, greeted)
     members_in = [exchange(pw_out, pw_in.at[d - 1], member(d)) for d in range(1, members)]
 
-    lane = lax.broadcasted_iota(jnp.int32, (rows, width), 1)
-    row = lax.broadcasted_iota(jnp.int32, (rows, width), 0)
-    inside_ha = ha_up.astype(jnp.float32)
-    inside_lat = lat_up.astype(jnp.float32)
-
-    def y_lower(v):
-        return jnp.where(lane == 0, 0.0, pltpu.roll(v, 1, 1))
-
-    def y_upper(v):
-        return jnp.where(lane == width - 1, 0.0, pltpu.roll(v, width - 1, 1))
-
-    def x_lower(v, edge):
-        return jnp.where(row == 0, edge, pltpu.roll(v, 1, 0))
-
-    def x_upper(v, edge):
-        return jnp.where(row == rows - 1, edge, pltpu.roll(v, rows - 1, 0))
-
-    def material(z):
-        label = lb[z]
-        eps = jnp.full((rows, width), eps_table[0], jnp.float32)
-        chi = jnp.full((rows, width), 3.0 * chi_table[0], jnp.float32)
-        for region in range(1, regions):
-            hit = label == region
-            eps = jnp.where(hit, eps_table[region], eps)
-            chi = jnp.where(hit, 3.0 * chi_table[region], chi)
-        return eps, chi
-
-    def lower_parts(src, z):
-        sx, sy, sz = src[0, z], src[1, z], src[2, z]
-        curl_x = sz - y_lower(sz) - sy
-        curl_y = sx - (sz - x_lower(sz, 0.0))
-        curl_z = sy - x_lower(sy, 0.0) - (sx - y_lower(sx))
-        if z > 0:
-            curl_x = curl_x + src[1, z - 1]
-            curl_y = curl_y - src[0, z - 1]
-        return curl_x, curl_y, curl_z
-
-    def both_parts(z):
-        eps, chi = material(z)
-        inner = [jnp.zeros((rows, width), jnp.float32) for _ in range(2)]
-        for c in range(comps):
-            f = field(last, c, z)
-            inverse = 1.0 / (eps + chi * f * f)
-            for i, value in enumerate((e[c, z] * inverse, wgrid[z] * f * inverse)):
-                ab[i, c, z] = value
-                inner[i] = inner[i] + value * f
-                if c > 0:
-                    slot = (2 * i + c - 1) * depth + z
-                    rlab_out[slot : slot + 1, :] = value[rows - 1 : rows]
-                if c == 0 and z == top:
-                    caab_out[i : i + 1, :] = value[0:1]
-                if c == 2 and z == 0:
-                    cbab_out[i : i + 1, :] = value[rows - 1 : rows]
-        return [jnp.where(lb[z] == 0, value, 0.0) for value in inner]
-
-    def both_curls(z):
-        for i in range(2):
-            curl = lower_parts(ab.at[i], z)
-            for c in range(comps):
-                value = -time_step * curl[c]
-                if i == 0:
-                    value = h0[c, z] + value
-                pab[i, c, z] = value
-                if z == 0 and c < 2:
-                    hzab_out[i, c] = value
-                if c > 0:
-                    slot = (2 * i + c - 1) * depth + z
-                    ruab_out[slot : slot + 1, :] = value[0:1]
-
-    loads[3].wait()
-    loads[4].wait()
-    loads[5].wait()
-    inner = [jnp.zeros((rows, width), jnp.float32) for _ in range(2)]
-    for z in [0] + list(range(top, 0, -1)):
-        inner = [old + more for old, more in zip(inner, both_parts(z))]
-        if z == 0:
-            both_curls(0)
-            zuab_in = exchange(hzab_out, zuab, (lat, ha_prev), ha_dn, ha_up)
-        if z == top:
-            zlab_in = exchange(ab.at[:, pl.ds(0, 2), top], zlab, (lat, ha_next), ha_up, ha_dn)
+    inner_b, (zub_in, zlb_in) = ends(part_b, 1)
+    for z in range(1, top):
+        inner_a = inner_a + part_a(z)
+        inner_b = inner_b + part_b(z)
     corner_a = (
         (lat_prev, ha_next),
         jnp.logical_and(lat_dn, ha_up),
@@ -340,7 +361,8 @@
     groups_in = [exchange(pw_sum, pw_all.at[d - 1], counterpart(d)) for d in range(1, groups)]
 
     for z in range(1, depth):
-        both_curls(z)
+        part_curl(0, z)
+        part_curl(1, z)
     ruab_in = exchange(ruab_out, ruab, (lat_prev, ha), lat_dn, lat_up)
 
     loads[6].wait()
@@ -445,7 +467,7 @@
         return arrivals
 
     gain = inverse_power[last : last + 1, :]
-    acc = inner[0] + gain * inner[1]
+    acc = inner_a + gain * inner_b
     for z in range(depth):
         for c in range(comps):
             magnetic(last)[c, z] = pab[0, c, z] + gain * pab[1, c, z]
@@ -454,25 +476,18 @@
         half = ref.shape[0] // 2
         return ref[pl.ds(0, half)] + gain * ref[pl.ds(half, half)]
 
+    if last == 0:
+        plane_in = send_plane(acc)
     for k in reversed(range(steps)):
         if k == last:
-            rl_in, ru_in, zl_in, zu_in, ca_in, cb_in = (
-                rlab_in,
-                ruab_in,
-                zlab_in,
-                zuab_in,
-                caab_in,
-                cbab_in,
-            )
+            rl_in, ru_in, ca_in, cb_in = rlab_in, ruab_in, caab_in, cbab_in
         else:
             kept = len(issued)
             rl_in, ca_in, cb_in = send_edges(k)
-            if k == 0:
-                plane_in = send_plane(acc)
             for z in range(1, depth):
                 lower_layer(k, z)
             ru_in = exchange(ru_out.at[k], ru.at[k], (lat_prev, ha), lat_dn, lat_up)
-            finish_sends(len(issued) - kept + 2)
+            finish_sends(len(issued) - kept + 1 + 3 * n_ha)
 
         if k == last:
             dens_lo_in()
@@ -526,10 +541,25 @@
         for z in range(1, top):
             acc = finish_layer(z, new[0, z + 1], new[1, z + 1], acc)
 
-        zl_in()
+        if k == 0:
+            for arrive in plane_in:
+                arrive()
+            whole = plane[...]
+            low = plane_lo[0]
+            high = plane_hi[0]
+            for d in range(1, n_ha):
+                whole = whole + plane_ha[d - 1]
+                low = low + plane_lo[d]
+                high = high + plane_hi[d]
+            product = jnp.concatenate([low, whole, high], 0) * deriv[...]
+            out_g[...] = filter_rows(product, rows)
+
         if k == last:
+            zla_in()
+            zlb_in()
             below_x, below_y = zlab[0, 0] + gain * zlab[1, 0], zlab[0, 1] + gain * zlab[1, 1]
         else:
+            zl_in()
             below_x, below_y = zl[k, 0], zl[k, 1]
         new[0, 0] = new[0, 0] - time_step * below_y
         new[1, 0] = new[1, 0] + time_step * below_x
@@ -537,15 +567,18 @@
             acc = finish_layer(0, new[0, 1], new[1, 1], acc)
             if k > 0:
                 lower_layer(k - 1, 0)
-                zu_next = send_bottom(k - 1)
-
-        zu_in()
+                if k > 1:
+                    zu_next = send_bottom(k - 1)
+
         cb_in()
         if k == last:
+            zua_in()
+            zub_in()
             above_x, above_y = zuab[0, 0] + gain * zuab[1, 0], zuab[0, 1] + gain * zuab[1, 1]
             own_x, own_y = ab[0, 0, top] + gain * ab[1, 0, top], ab[0, 1, top] + gain * ab[1, 1, top]
             corner = joined(cbab)
         else:
+            zu_in()
             above_x, above_y = zu[k, 0], zu[k, 1]
             own_x, own_y = s[k, 0, top], s[k, 1, top]
             corner = cb[k]
@@ -553,24 +586,16 @@
         above_y = above_y + time_step * own_x
         above_y = above_y - jnp.where(row == 0, time_step * corner, 0.0)
         acc = finish_layer(top, above_x * inside_ha, above_y * inside_ha, acc)
+        if k == 1:
+            plane_in = send_plane(acc)
         if k > 0:
             if top == 0:
                 lower_layer(k - 1, 0)
+            if top == 0 or k == 1:
                 zu_next = send_bottom(k - 1)
             zu_in = zu_next
             zl_in = send_top(k - 1)
 
-    for arrive in plane_in:
-        arrive()
-    middle = plane[...]
-    low = plane_lo[0]
-    high = plane_hi[0]
-    for d in range(1, n_ha):
-        middle = middle + plane_ha[d - 1]
-        low = low + plane_lo[d]
-        high = high + plane_hi[d]
-    product = jnp.concatenate([low, middle, high], 0) * deriv[...]
-    out_g[...] = filter_rows(product, rows)
     finish_sends()
 
 
@@ -596,10 +621,9 @@
     block = (comps, depth, rows, width)
     group = 2 if n_lat % 2 == 0 else 1
     members, groups = group * n_ha, n_lat // group
-    copies = (members - 1) + (groups - 1) + 2 + 6 * steps + 3 * n_ha - 1
+    copies = (members - 1) + (groups - 1) + 4 + 6 * steps + 3 * n_ha - 1
     vmem = pl.BlockSpec(memory_space=pltpu.VMEM)
     hbm = pl.BlockSpec(memory_space=pltpu.HBM)
-    scalars = pl.BlockSpec(memory_space=pltpu.SMEM)
     scratch = [
         pltpu.VMEM(block, f32),
         pltpu.VMEM(block, f32),
@@ -627,6 +651,8 @@
         pltpu.VMEM((steps, 1, width), f32),
         pltpu.VMEM((steps, 1, width), f32),
         pltpu.VMEM((steps, 1, width), f32),
+        pltpu.SMEM(eps_table.shape, f32),
+        pltpu.SMEM(chi_table.shape, f32),
         pltpu.VMEM((steps, width), f32),
         pltpu.VMEM((max(members - 1, 1), steps, width), f32),
         pltpu.VMEM((steps, width), f32),
@@ -647,7 +673,7 @@
         pltpu.VMEM((max(n_ha - 1, 1), rows, width), f32),
         pltpu.VMEM((n_ha, RADIUS, width), f32),
         pltpu.VMEM((n_ha, RADIUS, width), f32),
-        pltpu.SemaphoreType.DMA((7,)),
+        pltpu.SemaphoreType.DMA((9,)),
         pltpu.SemaphoreType.DMA((copies,)),
         pltpu.SemaphoreType.DMA((copies,)),
     ]
@@ -658,7 +684,7 @@
             pltpu.VMEM(block, f32),
             pltpu.VMEM((rows, width), f32),
         ),
-        in_specs=[hbm] * 4 + [scalars] * 2 + [hbm] * 3,
+        in_specs=[hbm] * 9,
         out_specs=(vmem, vmem, vmem),
         scratch_shapes=scratch,
         compiler_params=pltpu.CompilerParams(

time: 20.1 us -> 20.4 us (1.015)
  the two profiles are of different devices: /device:TPU:1 before, /device:TPU:0 now
where the time goes in v5:
time: 20.4 us; the launch traced here: 20.3 us
  Pallas kernels  19.6 us (96%)
  between operations  0.64 us (3%)
    pallas_call x1, Pallas kernels, body(): pl.pallas_call(functools.partial(kernel, n_lat, n_ha), out_shape=(pltpu.V...  18.7 us
    pallas_call x1, Pallas kernels, body(): pl.pallas_call(store, out_shape=(jax.ShapeDtypeStruct(block, f32), jax.Sh...  0.91 us

profile of v5, /device:TPU:0, one launch (start us, length us, event | category | flops | bytes accessed | tf_op | source)
XLA Modules:
  0.0 20.3 jit_solution(131004818000803874)
XLA Ops:
  0.6 18.7 %shard_map.112 = (f32[3,4,64,128]{3,2,1,0:T(8,128)S(1)}, f32[3,4,64,128]{3,2,1,0:T(8,128)S(1)}, f32[64,128]{1,0:T(8,128)S(1)}) custom-call(f32[3,4,64,128]{3,2,1,0:T(8,128)} %adj_e.1, f32[3,4,64,128]{3,2,1,0:T(8,128)} %adj_h.1, bf16[2,3,4,64,128]{4,3,2,1,0:T(8,128)(2,1)} %saved.1, s32[4,64,128]{2,1,0:T(8,128)} %labels.1, f32[4]{0:T(128)} %eps_table.1, ...), custom_call_target="tpu_custom_call" | custom-call | tf_op jit(solution)/shard_map/pallas_call | solution.py:680
  19.4 0.9 %shard_map.113 = (f32[3,4,64,128]{3,2,1,0:T(8,128)}, f32[3,4,64,128]{3,2,1,0:T(8,128)}, f32[64,128]{1,0:T(8,128)}) custom-call(f32[3,4,64,128]{3,2,1,0:T(8,128)S(1)} %get-tuple-element.6.e, f32[3,4,64,128]{3,2,1,0:T(8,128)S(1)} %get-tuple-element.7.h, f32[64,128]{1,0:T(8,128)S(1)} %get-tuple-element.8.g), custom_call_target="tpu_custom_call" | custom-call | tf_op jit(solution)/shard_map/pallas_call | solution.py:704

commit v6 on v5

--- a/solution.py
+++ b/solution.py
@@ -283,11 +283,9 @@
                 slot = (2 * i + c - 1) * depth + z
                 ruab_out[slot : slot + 1, :] = value[0:1]
 
-    def ends(part, i, wait=None):
+    def ends(part, i):
         inner = part(0)
         part_curl(i, 0)
-        if wait is not None:
-            wait()
         arrivals = [exchange(hzab_out.at[i], zuab.at[i], (lat, ha_prev), ha_dn, ha_up)]
         if top > 0:
             inner = inner + part(top)
@@ -295,12 +293,6 @@
             exchange(ab.at[i, pl.ds(0, 2), top], zlab.at[i], (lat, ha_next), ha_up, ha_dn)
         )
         return inner, arrivals
-
-    for index in (2, 3, 4, 5, 7, 8):
-        loads[index].wait()
-    inner_a, (zua_in, zla_in) = ends(
-        part_a, 0, lambda: pl.semaphore_wait(barrier, greeted)
-    )
 
     loads[0].wait()
     loads[1].wait()
@@ -322,6 +314,7 @@
     for z in range(depth):
         wgrid[z] = total[z * rows : (z + 1) * rows]
 
+    loads[2].wait()
     for k in range(steps):
         acc = jnp.zeros((rows, width), jnp.float32)
         for z in range(depth):
@@ -332,8 +325,12 @@
             acc = acc + wgrid[z] * square
         pw_out[k : k + 1, :] = jnp.sum(acc, 0, keepdims=True)
 
+    pl.semaphore_wait(barrier, greeted)
     members_in = [exchange(pw_out, pw_in.at[d - 1], member(d)) for d in range(1, members)]
 
+    for index in (3, 4, 5, 7, 8):
+        loads[index].wait()
+    inner_a, (zua_in, zla_in) = ends(part_a, 0)
     inner_b, (zub_in, zlb_in) = ends(part_b, 1)
     for z in range(1, top):
         inner_a = inner_a + part_a(z)
@@ -442,10 +439,8 @@
     def send_plane(acc):
         plane[...] = acc
         arrivals = []
-        for d in range(n_ha):
+        for d in reversed(range(n_ha)):
             other = lax.rem(ha + d, n_ha)
-            if d > 0:
-                arrivals.append(exchange(plane, plane_ha.at[d - 1], (lat, other)))
             arrivals.append(
                 exchange(
                     plane.at[pl.ds(rows - RADIUS, RADIUS)],
@@ -464,6 +459,8 @@
                     lat_up,
                 )
             )
+        for d in range(1, n_ha):
+            arrivals.append(exchange(plane, plane_ha.at[d - 1], (lat, lax.rem(ha + d, n_ha))))
         return arrivals
 
     gain = inverse_power[last : last + 1, :]
@@ -541,19 +538,6 @@
         for z in range(1, top):
             acc = finish_layer(z, new[0, z + 1], new[1, z + 1], acc)
 
-        if k == 0:
-            for arrive in plane_in:
-                arrive()
-            whole = plane[...]
-            low = plane_lo[0]
-            high = plane_hi[0]
-            for d in range(1, n_ha):
-                whole = whole + plane_ha[d - 1]
-                low = low + plane_lo[d]
-                high = high + plane_hi[d]
-            product = jnp.concatenate([low, whole, high], 0) * deriv[...]
-            out_g[...] = filter_rows(product, rows)
-
         if k == last:
             zla_in()
             zlb_in()
@@ -567,8 +551,7 @@
             acc = finish_layer(0, new[0, 1], new[1, 1], acc)
             if k > 0:
                 lower_layer(k - 1, 0)
-                if k > 1:
-                    zu_next = send_bottom(k - 1)
+                zu_next = send_bottom(k - 1)
 
         cb_in()
         if k == last:
@@ -586,16 +569,26 @@
         above_y = above_y + time_step * own_x
         above_y = above_y - jnp.where(row == 0, time_step * corner, 0.0)
         acc = finish_layer(top, above_x * inside_ha, above_y * inside_ha, acc)
-        if k == 1:
-            plane_in = send_plane(acc)
         if k > 0:
             if top == 0:
                 lower_layer(k - 1, 0)
-            if top == 0 or k == 1:
                 zu_next = send_bottom(k - 1)
             zu_in = zu_next
             zl_in = send_top(k - 1)
-
+        if k == 1:
+            plane_in = send_plane(acc)
+
+    for arrive in plane_in:
+        arrive()
+    whole = plane[...]
+    low = plane_lo[0]
+    high = plane_hi[0]
+    for d in range(1, n_ha):
+        whole = whole + plane_ha[d - 1]
+        low = low + plane_lo[d]
+        high = high + plane_hi[d]
+    product = jnp.concatenate([low, whole, high], 0) * deriv[...]
+    out_g[...] = filter_rows(product, rows)
     finish_sends()
 
 

time: 20.4 us -> 19.3 us (0.946)
  Pallas kernels: 19.6 us -> 18.5 us
    pallas_call x1, Pallas kernels: 18.7 us -> 17.6 us  [body(): pl.pallas_call(functools.partial(kernel, n_lat, n_ha), out_shape=(pltpu.V...]
where the time goes in v6:
time: 19.3 us; the launch traced here: 19.1 us
  Pallas kernels  18.5 us (96%)
  between operations  0.64 us (3%)
    pallas_call x1, Pallas kernels, body(): pl.pallas_call(functools.partial(kernel, n_lat, n_ha), out_shape=(pltpu.V...  17.6 us
    pallas_call x1, Pallas kernels, body(): pl.pallas_call(store, out_shape=(jax.ShapeDtypeStruct(block, f32), jax.Sh...  0.91 us

profile of v6, /device:TPU:0, one launch (start us, length us, event | category | flops | bytes accessed | tf_op | source)
XLA Modules:
  0.0 19.1 jit_solution(5669121351399579252)
XLA Ops:
  0.6 17.6 %shard_map.112 = (f32[3,4,64,128]{3,2,1,0:T(8,128)S(1)}, f32[3,4,64,128]{3,2,1,0:T(8,128)S(1)}, f32[64,128]{1,0:T(8,128)S(1)}) custom-call(f32[3,4,64,128]{3,2,1,0:T(8,128)} %adj_e.1, f32[3,4,64,128]{3,2,1,0:T(8,128)} %adj_h.1, bf16[2,3,4,64,128]{4,3,2,1,0:T(8,128)(2,1)} %saved.1, s32[4,64,128]{2,1,0:T(8,128)} %labels.1, f32[4]{0:T(128)} %eps_table.1, ...), custom_call_target="tpu_custom_call" | custom-call | tf_op jit(solution)/shard_map/pallas_call | solution.py:673
  18.2 0.9 %shard_map.113 = (f32[3,4,64,128]{3,2,1,0:T(8,128)}, f32[3,4,64,128]{3,2,1,0:T(8,128)}, f32[64,128]{1,0:T(8,128)}) custom-call(f32[3,4,64,128]{3,2,1,0:T(8,128)S(1)} %get-tuple-element.6.e, f32[3,4,64,128]{3,2,1,0:T(8,128)S(1)} %get-tuple-element.7.h, f32[64,128]{1,0:T(8,128)S(1)} %get-tuple-element.8.g), custom_call_target="tpu_custom_call" | custom-call | tf_op jit(solution)/shard_map/pallas_call | solution.py:697

commit v7 on v6

--- a/solution.py
+++ b/solution.py
@@ -17,24 +17,28 @@
 MESH = pl.DeviceIdType.MESH
 
 
-def cone(offset):
-    return jnp.maximum(RADIUS + 1 - jnp.abs(offset), 0).astype(jnp.float32) / (RADIUS + 1) ** 2
-
-
-def filter_rows(padded, rows):
-    width = padded.shape[1]
-    i = lax.broadcasted_iota(jnp.int32, (width, width), 0)
-    j = lax.broadcasted_iota(jnp.int32, (width, width), 1)
-    smoothed = jnp.dot(
-        padded, cone(i - j), precision=lax.Precision.HIGHEST, preferred_element_type=jnp.float32
+def cone(shape, shift):
+    offset = lax.broadcasted_iota(jnp.int32, shape, 1) - lax.broadcasted_iota(jnp.int32, shape, 0)
+    weights = jnp.maximum(RADIUS + 1 - jnp.abs(offset - shift), 0)
+    return weights.astype(jnp.float32).astype(jnp.bfloat16)
+
+
+def pieces(value):
+    first = value.astype(jnp.bfloat16)
+    left = value - first.astype(jnp.float32)
+    second = left.astype(jnp.bfloat16)
+    third = (left - second.astype(jnp.float32)).astype(jnp.bfloat16)
+    return third, second, first
+
+
+def filter_rows(padded, across, downward):
+    scale = 1.0 / (RADIUS + 1) ** 2
+    smoothed = sum(
+        jnp.dot(part, across, preferred_element_type=jnp.float32) for part in pieces(padded)
     )
-    row_out = lax.broadcasted_iota(jnp.int32, (rows, rows + 2 * RADIUS), 0)
-    row_in = lax.broadcasted_iota(jnp.int32, (rows, rows + 2 * RADIUS), 1)
-    return jnp.dot(
-        cone(row_in - RADIUS - row_out),
-        smoothed,
-        precision=lax.Precision.HIGHEST,
-        preferred_element_type=jnp.float32,
+    return scale * sum(
+        jnp.dot(downward, part, preferred_element_type=jnp.float32)
+        for part in pieces(scale * smoothed)
     )
 
 
@@ -81,6 +85,9 @@
     cb,
     eps_of,
     chi_of,
+    cone_y,
+    cone_x,
+    cone_wide,
     pw_out,
     pw_in,
     pw_sum,
@@ -265,9 +272,9 @@
             slot = (2 * i + c - 1) * depth + z
             rlab_out[slot : slot + 1, :] = value[rows - 1 : rows]
         if c == 0 and z == top:
-            caab_out[i : i + 1, :] = value[0:1]
+            caab_out[i] = value[0:1]
         if c == 2 and z == 0:
-            cbab_out[i : i + 1, :] = value[rows - 1 : rows]
+            cbab_out[i] = value[rows - 1 : rows]
         return value
 
     def part_curl(i, z):
@@ -286,27 +293,31 @@
     def ends(part, i):
         inner = part(0)
         part_curl(i, 0)
-        arrivals = [exchange(hzab_out.at[i], zuab.at[i], (lat, ha_prev), ha_dn, ha_up)]
+        arrivals = [
+            exchange(cbab_out.at[i], cbab.at[i], *corner_b),
+            exchange(hzab_out.at[i], zuab.at[i], (lat, ha_prev), ha_dn, ha_up),
+        ]
         if top > 0:
             inner = inner + part(top)
+        arrivals.append(exchange(caab_out.at[i], caab.at[i], *corner_a))
         arrivals.append(
             exchange(ab.at[i, pl.ds(0, 2), top], zlab.at[i], (lat, ha_next), ha_up, ha_dn)
         )
         return inner, arrivals
 
+    cone_y[...] = cone(cone_y.shape, 0)
+    cone_x[...] = cone(cone_x.shape, RADIUS)
+    cone_wide[...] = cone(cone_wide.shape, RADIUS)
+
     loads[0].wait()
     loads[1].wait()
     cell = cl[...]
     amount = wt[...]
-    first = amount.astype(jnp.bfloat16)
-    left = amount - first.astype(jnp.float32)
-    second = left.astype(jnp.bfloat16)
-    third = (left - second.astype(jnp.float32)).astype(jnp.bfloat16)
     line = lax.broadcasted_iota(jnp.int32, (depth * rows, entries), 0) == cell // width
     lane_hit = lax.broadcasted_iota(jnp.int32, (width, entries), 0) == lax.rem(cell, width)
     line = jnp.where(line, 1.0, 0.0).astype(jnp.bfloat16)
     total = jnp.zeros((depth * rows, width), jnp.float32)
-    for part in (third, second, first):
+    for part in pieces(amount):
         spread = jnp.where(lane_hit, part.astype(jnp.float32), 0.0).astype(jnp.bfloat16)
         total = total + lax.dot_general(
             line, spread, (((1,), (1,)), ((), ())), preferred_element_type=jnp.float32
@@ -328,13 +339,6 @@
     pl.semaphore_wait(barrier, greeted)
     members_in = [exchange(pw_out, pw_in.at[d - 1], member(d)) for d in range(1, members)]
 
-    for index in (3, 4, 5, 7, 8):
-        loads[index].wait()
-    inner_a, (zua_in, zla_in) = ends(part_a, 0)
-    inner_b, (zub_in, zlb_in) = ends(part_b, 1)
-    for z in range(1, top):
-        inner_a = inner_a + part_a(z)
-        inner_b = inner_b + part_b(z)
     corner_a = (
         (lat_prev, ha_next),
         jnp.logical_and(lat_dn, ha_up),
@@ -345,9 +349,14 @@
         jnp.logical_and(lat_up, ha_dn),
         jnp.logical_and(lat_dn, ha_up),
     )
+    for index in (3, 4, 5, 7, 8):
+        loads[index].wait()
+    inner_a, (cba_in, zua_in, caa_in, zla_in) = ends(part_a, 0)
+    inner_b, (cbb_in, zub_in, cab_in, zlb_in) = ends(part_b, 1)
+    for z in range(1, top):
+        inner_a = inner_a + part_a(z)
+        inner_b = inner_b + part_b(z)
     rlab_in = exchange(rlab_out, rlab, (lat_next, ha), lat_up, lat_dn)
-    caab_in = exchange(caab_out, caab, *corner_a)
-    cbab_in = exchange(cbab_out, cbab, *corner_b)
 
     for arrive in members_in:
         arrive()
@@ -424,16 +433,15 @@
                 ru_out[k, slot : slot + 1, :] = values[c][0:1]
 
     def send_bottom(k):
-        return exchange(hz_out.at[k], zu.at[k], (lat, ha_prev), ha_dn, ha_up)
+        return (
+            exchange(cb_out.at[k], cb.at[k], *corner_b),
+            exchange(hz_out.at[k], zu.at[k], (lat, ha_prev), ha_dn, ha_up),
+        )
 
     def send_top(k):
-        return exchange(s.at[k, pl.ds(0, 2), top], zl.at[k], (lat, ha_next), ha_up, ha_dn)
-
-    def send_edges(k):
         return (
-            exchange(rl_out.at[k], rl.at[k], (lat_next, ha), lat_up, lat_dn),
             exchange(ca_out.at[k], ca.at[k], *corner_a),
-            exchange(cb_out.at[k], cb.at[k], *corner_b),
+            exchange(s.at[k, pl.ds(0, 2), top], zl.at[k], (lat, ha_next), ha_up, ha_dn),
         )
 
     def send_plane(acc):
@@ -477,20 +485,20 @@
         plane_in = send_plane(acc)
     for k in reversed(range(steps)):
         if k == last:
-            rl_in, ru_in, ca_in, cb_in = rlab_in, ruab_in, caab_in, cbab_in
+            rl_in, ru_in = rlab_in, ruab_in
         else:
             kept = len(issued)
-            rl_in, ca_in, cb_in = send_edges(k)
+            rl_in = exchange(rl_out.at[k], rl.at[k], (lat_next, ha), lat_up, lat_dn)
             for z in range(1, depth):
                 lower_layer(k, z)
             ru_in = exchange(ru_out.at[k], ru.at[k], (lat_prev, ha), lat_dn, lat_up)
-            finish_sends(len(issued) - kept + 1 + 3 * n_ha)
+            finish_sends(len(issued) - kept + 3 + 3 * n_ha)
 
         if k == last:
             dens_lo_in()
             dens_hi_in()
             extended = jnp.concatenate([dens_lo[...], dens[...], dens_hi[...]], 0)
-            filtered = filter_rows(extended, rows + 2 * RADIUS)
+            filtered = filter_rows(extended, cone_y[...], cone_wide[...])
             slope = jnp.tanh(sharpness * (filtered - threshold))
             deriv[...] = (
                 sharpness
@@ -506,10 +514,14 @@
             new[2, z, 0:1] = new[2, z, 0:1] + time_step * low[z : z + 1]
 
         ru_in()
-        ca_in()
+        if k == last:
+            caa_in()
+            cab_in()
+        else:
+            ca_in()
         own = joined(rlab_out) if k == last else rl_out[k]
         high = joined(ruab) if k == last else ru[k]
-        corner = joined(caab) if k == last else ca[k]
+        corner = caab[0] + gain * caab[1] if k == last else ca[k]
         high_y = (high[0:depth] - time_step * own[depth : 2 * depth]) * inside_lat
         high_z = (high[depth : 2 * depth] + time_step * own[0:depth]) * inside_lat
         first_y = high_y[0:1] + time_step * inside_lat * corner
@@ -551,16 +563,18 @@
             acc = finish_layer(0, new[0, 1], new[1, 1], acc)
             if k > 0:
                 lower_layer(k - 1, 0)
-                zu_next = send_bottom(k - 1)
-
-        cb_in()
+                cb_next, zu_next = send_bottom(k - 1)
+
         if k == last:
+            cba_in()
+            cbb_in()
             zua_in()
             zub_in()
             above_x, above_y = zuab[0, 0] + gain * zuab[1, 0], zuab[0, 1] + gain * zuab[1, 1]
             own_x, own_y = ab[0, 0, top] + gain * ab[1, 0, top], ab[0, 1, top] + gain * ab[1, 1, top]
-            corner = joined(cbab)
+            corner = cbab[0] + gain * cbab[1]
         else:
+            cb_in()
             zu_in()
             above_x, above_y = zu[k, 0], zu[k, 1]
             own_x, own_y = s[k, 0, top], s[k, 1, top]
@@ -572,12 +586,13 @@
         if k > 0:
             if top == 0:
                 lower_layer(k - 1, 0)
-                zu_next = send_bottom(k - 1)
-            zu_in = zu_next
-            zl_in = send_top(k - 1)
+                cb_next, zu_next = send_bottom(k - 1)
+            cb_in, zu_in = cb_next, zu_next
+            ca_in, zl_in = send_top(k - 1)
         if k == 1:
             plane_in = send_plane(acc)
 
+    finish_sends()
     for arrive in plane_in:
         arrive()
     whole = plane[...]
@@ -588,8 +603,7 @@
         low = low + plane_lo[d]
         high = high + plane_hi[d]
     product = jnp.concatenate([low, whole, high], 0) * deriv[...]
-    out_g[...] = filter_rows(product, rows)
-    finish_sends()
+    out_g[...] = filter_rows(product, cone_y[...], cone_x[...])
 
 
 def store(e, h, g, out_e, out_h, out_g, sem):
@@ -614,7 +628,7 @@
     block = (comps, depth, rows, width)
     group = 2 if n_lat % 2 == 0 else 1
     members, groups = group * n_ha, n_lat // group
-    copies = (members - 1) + (groups - 1) + 4 + 6 * steps + 3 * n_ha - 1
+    copies = (members - 1) + (groups - 1) + 6 + 6 * steps + 3 * n_ha - 1
     vmem = pl.BlockSpec(memory_space=pltpu.VMEM)
     hbm = pl.BlockSpec(memory_space=pltpu.HBM)
     scratch = [
@@ -646,6 +660,9 @@
         pltpu.VMEM((steps, 1, width), f32),
         pltpu.SMEM(eps_table.shape, f32),
         pltpu.SMEM(chi_table.shape, f32),
+        pltpu.VMEM((width, width), jnp.bfloat16),
+        pltpu.VMEM((rows, rows + 2 * RADIUS), jnp.bfloat16),
+        pltpu.VMEM((rows + 2 * RADIUS, rows + 4 * RADIUS), jnp.bfloat16),
         pltpu.VMEM((steps, width), f32),
         pltpu.VMEM((max(members - 1, 1), steps, width), f32),
         pltpu.VMEM((steps, width), f32),
@@ -659,10 +676,10 @@
         pltpu.VMEM((4 * depth, width), f32),
         pltpu.VMEM((4 * depth, width), f32),
         pltpu.VMEM((4 * depth, width), f32),
-        pltpu.VMEM((2, width), f32),
-        pltpu.VMEM((2, width), f32),
-        pltpu.VMEM((2, width), f32),
-        pltpu.VMEM((2, width), f32),
+        pltpu.VMEM((2, 1, width), f32),
+        pltpu.VMEM((2, 1, width), f32),
+        pltpu.VMEM((2, 1, width), f32),
+        pltpu.VMEM((2, 1, width), f32),
         pltpu.VMEM((max(n_ha - 1, 1), rows, width), f32),
         pltpu.VMEM((n_ha, RADIUS, width), f32),
         pltpu.VMEM((n_ha, RADIUS, width), f32),

time: 19.3 us -> 19.1 us (0.990)
  Pallas kernels: 18.5 us -> 18.3 us
where the time goes in v7:
time: 19.1 us; the launch traced here: 19 us
  Pallas kernels  18.3 us (96%)
  between operations  0.64 us (3%)
    pallas_call x1, Pallas kernels, body(): pl.pallas_call(functools.partial(kernel, n_lat, n_ha), out_shape=(pltpu.V...  17.4 us
    pallas_call x1, Pallas kernels, body(): pl.pallas_call(store, out_shape=(jax.ShapeDtypeStruct(block, f32), jax.Sh...  0.91 us

profile of v7, /device:TPU:0, one launch (start us, length us, event | category | flops | bytes accessed | tf_op | source)
XLA Modules:
  0.0 19.0 jit_solution(16788744546165829554)
XLA Ops:
  0.6 17.4 %shard_map.112 = (f32[3,4,64,128]{3,2,1,0:T(8,128)S(1)}, f32[3,4,64,128]{3,2,1,0:T(8,128)S(1)}, f32[64,128]{1,0:T(8,128)S(1)}) custom-call(f32[3,4,64,128]{3,2,1,0:T(8,128)} %adj_e.1, f32[3,4,64,128]{3,2,1,0:T(8,128)} %adj_h.1, bf16[2,3,4,64,128]{4,3,2,1,0:T(8,128)(2,1)} %saved.1, s32[4,64,128]{2,1,0:T(8,128)} %labels.1, f32[4]{0:T(128)} %eps_table.1, ...), custom_call_target="tpu_custom_call" | custom-call | tf_op jit(solution)/shard_map/pallas_call | solution.py:690
  18.0 0.9 %shard_map.113 = (f32[3,4,64,128]{3,2,1,0:T(8,128)}, f32[3,4,64,128]{3,2,1,0:T(8,128)}, f32[64,128]{1,0:T(8,128)}) custom-call(f32[3,4,64,128]{3,2,1,0:T(8,128)S(1)} %get-tuple-element.6.e, f32[3,4,64,128]{3,2,1,0:T(8,128)S(1)} %get-tuple-element.7.h, f32[64,128]{1,0:T(8,128)S(1)} %get-tuple-element.8.g), custom_call_target="tpu_custom_call" | custom-call | tf_op jit(solution)/shard_map/pallas_call | solution.py:714

commit v8 on v7

--- a/solution.py
+++ b/solution.py
@@ -386,6 +386,17 @@
                 f = field(k, c, z)
                 rinv[k, c, z] = 1.0 / (eps + chi * f * f)
 
+    dens_lo_in()
+    dens_hi_in()
+    extended = jnp.concatenate([dens_lo[...], dens[...], dens_hi[...]], 0)
+    filtered = filter_rows(extended, cone_y[...], cone_wide[...])
+    slope = jnp.tanh(sharpness * (filtered - threshold))
+    deriv[...] = (
+        sharpness
+        * (1.0 - slope * slope)
+        / (jnp.tanh(sharpness * threshold) + jnp.tanh(sharpness * (1.0 - threshold)))
+    )
+
     for arrive in groups_in:
         arrive()
     for d in range(1, groups):
@@ -494,18 +505,6 @@
             ru_in = exchange(ru_out.at[k], ru.at[k], (lat_prev, ha), lat_dn, lat_up)
             finish_sends(len(issued) - kept + 3 + 3 * n_ha)
 
-        if k == last:
-            dens_lo_in()
-            dens_hi_in()
-            extended = jnp.concatenate([dens_lo[...], dens[...], dens_hi[...]], 0)
-            filtered = filter_rows(extended, cone_y[...], cone_wide[...])
-            slope = jnp.tanh(sharpness * (filtered - threshold))
-            deriv[...] = (
-                sharpness
-                * (1.0 - slope * slope)
-                / (jnp.tanh(sharpness * threshold) + jnp.tanh(sharpness * (1.0 - threshold)))
-            )
-
         new = magnetic(k)
         rl_in()
         low = joined(rlab) if k == last else rl[k]
@@ -547,8 +546,9 @@
                 out_e[c, z] = fields[c]
             return acc
 
-        for z in range(1, top):
-            acc = finish_layer(z, new[0, z + 1], new[1, z + 1], acc)
+        if k == 0:
+            for z in range(1, top):
+                acc = finish_layer(z, new[0, z + 1], new[1, z + 1], acc)
 
         if k == last:
             zla_in()
@@ -589,6 +589,8 @@
                 cb_next, zu_next = send_bottom(k - 1)
             cb_in, zu_in = cb_next, zu_next
             ca_in, zl_in = send_top(k - 1)
+            for z in range(1, top):
+                acc = finish_layer(z, new[0, z + 1], new[1, z + 1], acc)
         if k == 1:
             plane_in = send_plane(acc)
 

time: 19.1 us -> 19.2 us (level)
  no operation moved by 1% of the time
where the time goes in v8:
time: 19.2 us; the launch traced here: 19 us
  Pallas kernels  18.3 us (95%)
  between operations  0.64 us (3%)
    pallas_call x1, Pallas kernels, body(): pl.pallas_call(functools.partial(kernel, n_lat, n_ha), out_shape=(pltpu.V...  17.4 us
    pallas_call x1, Pallas kernels, body(): pl.pallas_call(store, out_shape=(jax.ShapeDtypeStruct(block, f32), jax.Sh...  0.91 us

profile of v8, /device:TPU:0, one launch (start us, length us, event | category | flops | bytes accessed | tf_op | source)
XLA Modules:
  0.0 19.0 jit_solution(15568212533355869362)
XLA Ops:
  0.6 17.4 %shard_map.112 = (f32[3,4,64,128]{3,2,1,0:T(8,128)S(1)}, f32[3,4,64,128]{3,2,1,0:T(8,128)S(1)}, f32[64,128]{1,0:T(8,128)S(1)}) custom-call(f32[3,4,64,128]{3,2,1,0:T(8,128)} %adj_e.1, f32[3,4,64,128]{3,2,1,0:T(8,128)} %adj_h.1, bf16[2,3,4,64,128]{4,3,2,1,0:T(8,128)(2,1)} %saved.1, s32[4,64,128]{2,1,0:T(8,128)} %labels.1, f32[4]{0:T(128)} %eps_table.1, ...), custom_call_target="tpu_custom_call" | custom-call | tf_op jit(solution)/shard_map/pallas_call | solution.py:692
  18.1 0.9 %shard_map.113 = (f32[3,4,64,128]{3,2,1,0:T(8,128)}, f32[3,4,64,128]{3,2,1,0:T(8,128)}, f32[64,128]{1,0:T(8,128)}) custom-call(f32[3,4,64,128]{3,2,1,0:T(8,128)S(1)} %get-tuple-element.6.e, f32[3,4,64,128]{3,2,1,0:T(8,128)S(1)} %get-tuple-element.7.h, f32[64,128]{1,0:T(8,128)S(1)} %get-tuple-element.8.g), custom_call_target="tpu_custom_call" | custom-call | tf_op jit(solution)/shard_map/pallas_call | solution.py:716

commit v9 on v8

--- a/solution.py
+++ b/solution.py
@@ -353,11 +353,6 @@
         loads[index].wait()
     inner_a, (cba_in, zua_in, caa_in, zla_in) = ends(part_a, 0)
     inner_b, (cbb_in, zub_in, cab_in, zlb_in) = ends(part_b, 1)
-    for z in range(1, top):
-        inner_a = inner_a + part_a(z)
-        inner_b = inner_b + part_b(z)
-    rlab_in = exchange(rlab_out, rlab, (lat_next, ha), lat_up, lat_dn)
-
     for arrive in members_in:
         arrive()
     power_rows = pw_out[...]
@@ -365,6 +360,11 @@
         power_rows = power_rows + pw_in[d - 1]
     pw_sum[...] = power_rows
     groups_in = [exchange(pw_sum, pw_all.at[d - 1], counterpart(d)) for d in range(1, groups)]
+
+    for z in range(1, top):
+        inner_a = inner_a + part_a(z)
+        inner_b = inner_b + part_b(z)
+    rlab_in = exchange(rlab_out, rlab, (lat_next, ha), lat_up, lat_dn)
 
     for z in range(1, depth):
         part_curl(0, z)

time: 19.2 us -> 19.2 us (level)
  no operation moved by 1% of the time
where the time goes in v9:
time: 19.2 us; the launch traced here: 19 us
  Pallas kernels  18.4 us (96%)
  between operations  0.64 us (3%)
    pallas_call x1, Pallas kernels, body(): pl.pallas_call(functools.partial(kernel, n_lat, n_ha), out_shape=(pltpu.V...  17.5 us
    pallas_call x1, Pallas kernels, body(): pl.pallas_call(store, out_shape=(jax.ShapeDtypeStruct(block, f32), jax.Sh...  0.91 us

profile of v9, /device:TPU:0, one launch (start us, length us, event | category | flops | bytes accessed | tf_op | source)
XLA Modules:
  0.0 19.0 jit_solution(698990237861544163)
XLA Ops:
  0.6 17.5 %shard_map.112 = (f32[3,4,64,128]{3,2,1,0:T(8,128)S(1)}, f32[3,4,64,128]{3,2,1,0:T(8,128)S(1)}, f32[64,128]{1,0:T(8,128)S(1)}) custom-call(f32[3,4,64,128]{3,2,1,0:T(8,128)} %adj_e.1, f32[3,4,64,128]{3,2,1,0:T(8,128)} %adj_h.1, bf16[2,3,4,64,128]{4,3,2,1,0:T(8,128)(2,1)} %saved.1, s32[4,64,128]{2,1,0:T(8,128)} %labels.1, f32[4]{0:T(128)} %eps_table.1, ...), custom_call_target="tpu_custom_call" | custom-call | tf_op jit(solution)/shard_map/pallas_call | solution.py:692
  18.1 0.9 %shard_map.113 = (f32[3,4,64,128]{3,2,1,0:T(8,128)}, f32[3,4,64,128]{3,2,1,0:T(8,128)}, f32[64,128]{1,0:T(8,128)}) custom-call(f32[3,4,64,128]{3,2,1,0:T(8,128)S(1)} %get-tuple-element.6.e, f32[3,4,64,128]{3,2,1,0:T(8,128)S(1)} %get-tuple-element.7.h, f32[64,128]{1,0:T(8,128)S(1)} %get-tuple-element.8.g), custom_call_target="tpu_custom_call" | custom-call | tf_op jit(solution)/shard_map/pallas_call | solution.py:716
